TPU v7x, 256 devices: a whole 4x4x8 slice. The times are simulated.
256 devices in a mesh: dom: 32 (over x_lo, z, core), col: 8 (over x_hi, y).
Axes of the slice: x: 4 (x_hi: 2, x_lo: 2; x = x_hi * 2 + x_lo), y: 4, z: 8, core: 2. Of those that a mesh axis runs over, the one named last changes fastest.
Arguments:
- feats: bfloat16 [16384, 256], P('dom', 'col'), may hold values from -6 to 6
- w_first: bfloat16 [256, 256], replicated, may hold values from -0.375 to 0.375
- w_second: bfloat16 [256, 256], replicated, may hold values from -0.375 to 0.375
- block_cols: int32 [128, 32], P('dom'), may hold values from 0 to 127, as said below
- block_count: int32 [128], P('dom'), may hold values from 1 to 32
- block_vals: bfloat16 [128, 32, 128, 128], P('dom', 'col'), may hold values from -0.125 to 0.125
- cotangent: bfloat16 [16384, 256], P('dom', 'col'), may hold values from -6 to 6
Outputs:
- output: float32 [16384, 256], P('dom', 'col')
- grad_first: float32 [256, 256], P(None, 'col')
- grad_second: float32 [256, 256], P(None, 'col')
Inputs may be any that keep to these rules, and one draw needn't show every extreme that they name: Each row of block_cols names 32 different column blocks.
All inputs are finite; a program needn't handle non-finite values.
Results may differ from a plain program's by a relative error of at most 0.019.
Values may be sent and summed in bfloat16 or wider, within the bound.
A program may use at most 64 MiB of HBM per device.

v0:
```python
import jax
import jax.numpy as jnp
from jax import lax
from jax.sharding import Mesh
from jax.sharding import PartitionSpec as P

BLK = 128
DOM = ("dom_0", "dom_1", "dom_2")


def in_blocks(shard, dim, peers):
    before, after = (shard.shape[:dim], shard.shape[dim + 1 :])
    return jnp.moveaxis(shard.reshape(*before, peers, -1, *after), dim, 0)


def sum_by_chip(shard, chips, core, dim):
    sizes = (lax.axis_size(chips), lax.axis_size(core))
    pieces = in_blocks(shard, dim, sizes[0] * sizes[1])
    inside = pieces.shape[1:]
    pieces = pieces.reshape(*sizes, *inside).swapaxes(0, 1).reshape(-1, *inside)
    pieces = lax.psum_scatter(pieces, core, scatter_dimension=0, tiled=True)
    return lax.psum_scatter(pieces, chips, scatter_dimension=0, tiled=True)[0]


def joined_along(pieces, dim):
    shape = list(pieces.shape[1:])
    shape[dim] *= pieces.shape[0]
    return jnp.moveaxis(pieces, 0, dim).reshape(shape)


def sent_to_all(shard, axis):
    peers = lax.axis_size(axis)
    return lax.all_to_all(
        jnp.broadcast_to(shard[None], (peers, *shard.shape)), axis, 0, 0, tiled=True
    )


def gathered_copies(shard, axis, dim):
    return joined_along(sent_to_all(shard, axis), dim)


def over_copies(shard, axis):
    everything = sent_to_all(shard, axis)
    return jnp.sum(everything.astype(jnp.float32), axis=0)


def summed_on_arrival(shard, axis, dim):
    pieces = in_blocks(shard, dim, lax.axis_size(axis))
    arrived = lax.all_to_all(pieces, axis, split_axis=0, concat_axis=0, tiled=True)
    return arrived.sum(axis=0)


def silu_slope(value):
    sig = jax.nn.sigmoid(value)
    return sig + value * sig * (1.0 - sig)


def forward_fold(prod, cols, vals):
    rows, width = prod.shape
    piece = lax.all_gather(prod, DOM, axis=0, tiled=True)
    count_blocks = piece.shape[0] // BLK
    hit = (cols >= 0) & (cols < count_blocks)
    picked = piece.reshape(count_blocks, BLK, width)[jnp.clip(cols, 0, count_blocks - 1)]
    picked = jnp.where(hit[:, :, None, None], picked, jnp.zeros((), picked.dtype))
    contrib = jnp.einsum("rkij,rkjf->rif", vals, picked, preferred_element_type=jnp.float32)
    return contrib.reshape(rows, width)


def backward_scatter(grad, cols, vals):
    rows, width = grad.shape
    nblocks = rows // BLK
    products = jnp.einsum(
        "rkij,rif->rkjf",
        vals,
        grad.reshape(nblocks, BLK, width),
        preferred_element_type=jnp.float32,
    )
    count = rows * lax.axis_size(("dom_0", "dom_1")) * lax.axis_size("dom_2")
    count_blocks = count // BLK
    onehot = (cols[:, :, None] == jnp.arange(count_blocks)[None, None, :]).astype(jnp.float32)
    summed = jnp.einsum("rkp,rkjf->pjf", onehot, products, precision=lax.Precision.HIGHEST)
    return sum_by_chip(summed.reshape(count, width), ("dom_0", "dom_1"), "dom_2", 0)


def body(feats, w_first, w_second, block_cols, block_count, block_vals, cotangent):
    col_index = lax.axis_index("col")
    rows, narrow = feats.shape

    def widen(value):
        return gathered_copies(value, "col", 1)

    def weight_grad(full, back):
        return over_copies(
            jnp.dot(full.T, back, preferred_element_type=jnp.float32).astype(jnp.bfloat16), DOM
        ).astype(jnp.float32)

    all_vals = lax.all_gather(block_vals, "col", axis=1, tiled=True)
    slot_ids = jnp.arange(all_vals.shape[1])
    usable = slot_ids[None, :] < block_count[:, None]
    vals = jnp.where(usable[:, :, None, None], all_vals, jnp.zeros((), all_vals.dtype))

    def project(full, weight):
        weight_cols = lax.dynamic_slice_in_dim(weight, col_index * narrow, narrow, 1)
        return jnp.dot(full, weight_cols, preferred_element_type=jnp.float32).astype(jnp.bfloat16)

    def aggregate(prod):
        return forward_fold(prod, block_cols, vals)

    def transpose(grad):
        return backward_scatter(grad, block_cols, vals)

    full_input = widen(feats)
    first = aggregate(project(full_input, w_first))
    hidden = (first * jax.nn.sigmoid(first)).astype(jnp.bfloat16)
    full_hidden = widen(hidden)
    output = aggregate(project(full_hidden, w_second))
    back_second = transpose(cotangent).astype(jnp.bfloat16)
    grad_second = weight_grad(full_hidden, back_second)
    second_cols = lax.dynamic_slice_in_dim(w_second, col_index * narrow, narrow, 1)
    partial_hidden = jnp.dot(back_second, second_cols.T, preferred_element_type=jnp.float32)
    hidden_grad = summed_on_arrival(partial_hidden, "col", 1)
    act_grad = (hidden_grad * silu_slope(first)).astype(jnp.bfloat16)
    back_first = transpose(act_grad).astype(jnp.bfloat16)
    grad_first = weight_grad(full_input, back_first)
    return (output, grad_first, grad_second)


def solution(mesh):
    split = Mesh(
        mesh.devices.reshape(2, 8, 2, mesh.shape["col"]), ("dom_0", "dom_1", "dom_2", "col")
    )
    return jax.shard_map(
        body,
        mesh=split,
        in_specs=(
            P(DOM, "col"),
            P(),
            P(),
            P(DOM, None),
            P(DOM),
            P(DOM, "col", None, None),
            P(DOM, "col"),
        ),
        out_specs=(P(DOM, "col"), P(None, "col"), P(None, "col")),
        check_vma=False,
    )
```

profile of v0, /device:TPU:1, one launch (start us, length us, event | category | flops | bytes accessed | tf_op | source)
XLA Modules:
  0.0 338.5 jit_solution(4655881142837038771)
XLA Ops:
  8.0 0.0 copy-start
  8.0 0.0 copy-start.2
  8.0 0.0 all-gather.4.cloned.1.call-start
  8.1 0.7 all-gather.4.cloned.1.call-update
  8.8 0.0 reduce-scatter.5.cloned.1.call-start
  8.8 0.8 reshape.85
  9.6 0.7 iota_compare_fusion.1
  10.3 81.0 %all-gather.4.cloned.1.call-done = bf16[4,32,128,128]{3,2,1,0:T(8,128)(2,1)} async-done(((bf16[4,4,128,128]{3,2,1,0:T(8,128)(2,1)}), bf16[4,32,128,128]{3,2,1,0:T(8,128)(2,1)}) %all-gather.4.cloned.1.call-update) | async-done | bytes 4194320 | tf_op jit(solution)/shard_map/all_gather | solution.py:97
  91.3 2.9 fusion
  94.3 0.0 copy-done.2
  94.3 2.5 fusion.12
  96.7 2.1 reshape_reshape_reshape.6
  98.9 4.2 %copy.31 = f32[2,16,512,32]{2,3,1,0:T(8,128)} copy(f32[2,16,512,32]{2,0,1,3:T(2,128)} %bitcast.126) | data formatting | bytes 4194304 | tf_op jit(solution)/shard_map/transpose | solution.py:20
  103.0 0.0 reduce-scatter.5.cloned.1.call-update
  103.1 0.0 copy-done.3
  103.1 0.7 broadcast_in_dim.41
  103.8 3.4 %all-to-all-start = ((bf16[8,512,32]{1,2,0:T(8,128)(2,1)}), bf16[8,512,32]{1,2,0:T(8,128)(2,1)S(1)}, u32[]{:S(2)}, u32[]{:S(2)}) async-start(bf16[8,512,32]{1,2,0:T(8,128)(2,1)} %broadcast_in_dim.41), calls=%async_computation | async-start | bytes 524288 | tf_op jit(solution)/shard_map/all_to_all | solution.py:33
  107.2 0.0 all-gather.6.cloned.1.call-start
  107.3 7.5 %all-to-all-done = bf16[8,512,32]{1,2,0:T(8,128)(2,1)S(1)} async-done(((bf16[8,512,32]{1,2,0:T(8,128)(2,1)}), bf16[8,512,32]{1,2,0:T(8,128)(2,1)S(1)}, u32[]{:S(2)}, u32[]{:S(2)}) %all-to-all-start) | async-done | bytes 262176 | tf_op jit(solution)/shard_map/all_to_all | solution.py:33
  114.7 0.0 copy-done
  114.7 0.9 fusion.19
  115.6 0.0 all-gather.6.cloned.1.call-update
  115.6 0.0 reduce-scatter.7.cloned.1.call-start
  115.7 1.4 reduce-scatter.5.cloned.1.call-done
  117.1 0.0 reduce-scatter.7.cloned.1.call-update
  117.1 0.1 reshape.90
  117.2 0.1 constant_dynamic-slice_fusion
  117.3 61.9 %all-gather.6.cloned.1.call-done = bf16[16384,32]{0,1:T(8,128)(2,1)} async-done(((bf16[512,32]{0,1:T(8,128)(2,1)}), bf16[16384,32]{0,1:T(8,128)(2,1)}) %all-gather.6.cloned.1.call-update) | async-done | bytes 1048592 | tf_op jit(solution)/shard_map/all_gather | solution.py:60
  179.3 1.4 copy_bitcast_fusion.1
  180.7 0.8 gather_fusion
  181.4 0.0 reduce-scatter.7.cloned.1.call-done
  181.5 1.8 convolution_bitcast_fusion
  183.3 6.5 %all-to-all-start.2 = ((f32[8,512,32]{1,2,0:T(8,128)}), f32[8,512,32]{1,2,0:T(8,128)S(1)}, u32[]{:S(2)}, u32[]{:S(2)}) async-start(f32[8,512,32]{1,2,0:T(8,128)} %convolution_bitcast_fusion), calls=%async_computation.4 | async-start | bytes 1048576 | tf_op jit(solution)/shard_map/all_to_all | solution.py:49
  189.8 0.2 reduce-scatter.9.cloned.1.call-start
  190.0 3.3 fusion.3
  193.3 5.1 %all-to-all-done.2 = f32[8,512,32]{1,2,0:T(8,128)S(1)} async-done(((f32[8,512,32]{1,2,0:T(8,128)}), f32[8,512,32]{1,2,0:T(8,128)S(1)}, u32[]{:S(2)}, u32[]{:S(2)}) %all-to-all-start.2) | async-done | bytes 524320 | tf_op jit(solution)/shard_map/all_to_all | solution.py:49
  198.4 2.9 fusion.1
  201.4 2.5 fusion.15
  203.8 2.1 reshape_reshape_reshape.7
  206.0 4.2 %copy.34 = f32[16,2,512,32]{2,3,0,1:T(8,128)} copy(f32[16,2,512,32]{2,1,0,3:T(2,128)} %reshape_reshape_reshape.7) | data formatting | bytes 4194304 | tf_op jit(solution)/shard_map/reshape;reshape;reshape | solution.py:20
  210.1 0.0 reduce-scatter.9.cloned.1.call-update
  210.2 0.0 reduce-scatter.11.cloned.1.call-start
  210.2 20.2 %reduce-scatter.9.cloned.1.call-done = f32[16,512,32]{1,2,0:T(8,128)} async-done(((f32[32,512,32]{1,2,0:T(8,128)}), f32[16,512,32]{1,2,0:T(8,128)}) %reduce-scatter.9.cloned.1.call-update) | async-done | bytes 1048592 | tf_op jit(solution)/shard_map/reduce_scatter | solution.py:21
  230.4 0.0 reduce-scatter.11.cloned.1.call-update
  230.5 0.0 all-gather.8.cloned.1.call-start
  230.6 13.7 %all_to_all.25 = bf16[8,512,32]{1,2,0:T(8,128)(2,1)S(1)} all-to-all(bf16[8,512,32]{1,2,0:T(8,128)(2,1)S(1)} %broadcast_in_dim.71), channel_id=1, replica_groups=mesh['dom_0'=2,'dom_1'=8,'dom_2'=2,'col'=8] {'col'}, dimensions={0} | all-to-all | bytes 524288 | tf_op jit(solution)/shard_map/all_to_all | solution.py:33
  244.2 0.8 convolution_convert_fusion
  245.0 0.0 all-gather.8.cloned.1.call-update
  245.1 0.2 convolution_convert_fusion.2
  245.2 0.9 broadcast_in_dim.73
  246.2 9.2 %all-to-all-start.4 = ((bf16[32,256,32]{1,2,0:T(8,128)(2,1)}), bf16[32,256,32]{1,2,0:T(8,128)(2,1)S(1)}, u32[]{:S(2)}, u32[]{:S(2)}) async-start(bf16[32,256,32]{1,2,0:T(8,128)(2,1)} %broadcast_in_dim.73), calls=%async_computation.8 | async-start | bytes 1048576 | tf_op jit(solution)/shard_map/all_to_all | solution.py:33
  255.4 41.2 %reduce-scatter.11.cloned.1.call-done = f32[1,512,32]{1,2,0:T(8,128)} async-done(((f32[16,512,32]{1,2,0:T(8,128)}), f32[1,512,32]{1,2,0:T(8,128)}) %reduce-scatter.11.cloned.1.call-update) | async-done | bytes 65552 | tf_op jit(solution)/shard_map/reduce_scatter | solution.py:22
  296.6 1.0 fusion.20
  297.6 0.0 all-to-all-done.4
  297.6 0.9 broadcast_in_dim.72
  298.5 15.4 %all-to-all-start.3 = ((bf16[32,256,32]{1,2,0:T(8,128)(2,1)}), bf16[32,256,32]{1,2,0:T(8,128)(2,1)S(1)}, u32[]{:S(2)}, u32[]{:S(2)}) async-start(bf16[32,256,32]{1,2,0:T(8,128)(2,1)} %broadcast_in_dim.72), calls=%async_computation.7 | async-start | bytes 1048576 | tf_op jit(solution)/shard_map/all_to_all | solution.py:33
  314.0 0.0 all-gather.8.cloned.1.call-done
  314.0 1.4 copy_bitcast_fusion
  315.4 0.8 gather_fusion.1
  316.2 3.3 fusion.18
  319.5 0.6 copy.68
  320.2 0.7 convert_reduce_fusion
  320.9 9.8 %all-to-all-done.3 = bf16[32,256,32]{1,2,0:T(8,128)(2,1)S(1)} async-done(((bf16[32,256,32]{1,2,0:T(8,128)(2,1)}), bf16[32,256,32]{1,2,0:T(8,128)(2,1)S(1)}, u32[]{:S(2)}, u32[]{:S(2)}) %all-to-all-start.3) | async-done | bytes 524320 | tf_op jit(solution)/shard_map/all_to_all | solution.py:33
  330.7 0.7 convert_reduce_fusion.1
  (11 shorter events, 0.1 us)
Async XLA Ops:
  8.0 106.7 %copy-start = (bf16[256,256]{1,0:T(8,128)(2,1)S(1)}, bf16[256,256]{1,0:T(8,128)(2,1)}, u32[]{:S(2)}) copy-start(bf16[256,256]{1,0:T(8,128)(2,1)} %param.8) | copy-start | bytes 393220
  8.0 86.2 %copy-start.2 = (s32[4,32]{1,0:T(4,128)S(1)}, s32[4,32]{1,0:T(4,128)}, u32[]{:S(2)}) copy-start(s32[4,32]{1,0:T(4,128)} %param.10) | copy-start | bytes 1540
  8.0 83.3 %all-gather.4.cloned.1.call-start = ((), (), s32[]{:S(2)}) async-start(), calls=%async_computation.9 | async-start | bytes 4718592 | tf_op jit(solution)/shard_map/all_gather | solution.py:97
  8.8 108.3 %reduce-scatter.5.cloned.1.call-start = ((), (), s32[]{:S(2)}) async-start(), calls=%async_computation.12 | async-start | bytes 3145728 | tf_op jit(solution)/shard_map/reduce_scatter | solution.py:21
  98.9 4.2 %copy-start.3 = (bf16[512,32]{0,1:T(8,128)(2,1)S(1)}, bf16[512,32]{0,1:T(8,128)(2,1)}, u32[]{:S(2)}) copy-start(bf16[512,32]{0,1:T(8,128)(2,1)} %param.7) | copy-start | bytes 98308
  98.9 18.4 %copy-start.4 = (bf16[256,256]{1,0:T(8,128)(2,1)S(1)}, bf16[256,256]{1,0:T(8,128)(2,1)}, u32[]{:S(2)}) copy-start(bf16[256,256]{1,0:T(8,128)(2,1)} %param.9) | copy-start | bytes 393220
  103.8 10.9 %all-to-all-start = ((bf16[8,512,32]{1,2,0:T(8,128)(2,1)}), bf16[8,512,32]{1,2,0:T(8,128)(2,1)S(1)}, u32[]{:S(2)}, u32[]{:S(2)}) async-start(bf16[8,512,32]{1,2,0:T(8,128)(2,1)} %broadcast_in_dim.41), calls=%async_computation | async-start | bytes 524288 | tf_op jit(solution)/shard_map/all_to_all | solution.py:33
  107.2 72.1 %all-gather.6.cloned.1.call-start = ((), (), s32[]{:S(2)}) async-start(), calls=%async_computation.10 | async-start | bytes 1081344 | tf_op jit(solution)/shard_map/all_gather | solution.py:60
  115.6 65.8 %reduce-scatter.7.cloned.1.call-start = ((), (), s32[]{:S(2)}) async-start(), calls=%async_computation.13 | async-start | bytes 1114112 | tf_op jit(solution)/shard_map/reduce_scatter | solution.py:22
  183.3 15.1 %all-to-all-start.2 = ((f32[8,512,32]{1,2,0:T(8,128)}), f32[8,512,32]{1,2,0:T(8,128)S(1)}, u32[]{:S(2)}, u32[]{:S(2)}) async-start(f32[8,512,32]{1,2,0:T(8,128)} %convolution_bitcast_fusion), calls=%async_computation.4 | async-start | bytes 1048576 | tf_op jit(solution)/shard_map/all_to_all | solution.py:49
  189.8 40.7 %reduce-scatter.9.cloned.1.call-start = ((), (), s32[]{:S(2)}) async-start(), calls=%async_computation.14 | async-start | bytes 3145728 | tf_op jit(solution)/shard_map/reduce_scatter | solution.py:21
  206.0 39.1 %copy-start.1 = (f32[1,512,32]{1,2,0:T(8,128)S(1)}, f32[1,512,32]{1,2,0:T(8,128)}, u32[]{:S(2)}) copy-start(f32[1,512,32]{1,2,0:T(8,128)} %reduce-scatter.7.cloned.1.call-done) | copy-start | bytes 196612
  210.2 86.5 %reduce-scatter.11.cloned.1.call-start = ((), (), s32[]{:S(2)}) async-start(), calls=%async_computation.15 | async-start | bytes 1114112 | tf_op jit(solution)/shard_map/reduce_scatter | solution.py:22
  230.5 83.5 %all-gather.8.cloned.1.call-start = ((), (), s32[]{:S(2)}) async-start(), calls=%async_computation.11 | async-start | bytes 1081344 | tf_op jit(solution)/shard_map/all_gather | solution.py:60
  246.2 51.5 %all-to-all-start.4 = ((bf16[32,256,32]{1,2,0:T(8,128)(2,1)}), bf16[32,256,32]{1,2,0:T(8,128)(2,1)S(1)}, u32[]{:S(2)}, u32[]{:S(2)}) async-start(bf16[32,256,32]{1,2,0:T(8,128)(2,1)} %broadcast_in_dim.73), calls=%async_computation.8 | async-start | bytes 1048576 | tf_op jit(solution)/shard_map/all_to_all | solution.py:33
  298.5 32.2 %all-to-all-start.3 = ((bf16[32,256,32]{1,2,0:T(8,128)(2,1)}), bf16[32,256,32]{1,2,0:T(8,128)(2,1)S(1)}, u32[]{:S(2)}, u32[]{:S(2)}) async-start(bf16[32,256,32]{1,2,0:T(8,128)(2,1)} %broadcast_in_dim.72), calls=%async_computation.7 | async-start | bytes 1048576 | tf_op jit(solution)/shard_map/all_to_all | solution.py:33
Sparse Core Ops, SparseCore 0:
  11.4 79.8 all-gather.3
  103.2 13.8 reduce-scatter.4
  119.8 61.4 reduce-scatter.6
  210.3 20.1 reduce-scatter.8
  232.9 63.6 reduce-scatter.10
Sparse Core Ops, SparseCore 1:
  115.7 63.5 all-gather.5
  245.1 66.9 all-gather.7
where the time goes:
time: 340 us; the launch traced here: 339 us
  waiting for transfers between devices  229 us (67%)
  starting transfers between devices  35 us (10%)
  matrix products  22.1 us (6%)
  local copies, waits for them, and re-layouts  21.1 us (6%)
  between operations  15.4 us (5%)
  blocking collectives  13.7 us (4%)
    all_gather x1, waiting for transfers between devices, body(): all_vals = lax.all_gather(block_vals, 'col', axis=1, tiled=True)  81 us
    all_gather x2, waiting for transfers between devices, forward_fold(): piece = lax.all_gather(prod, DOM, axis=0, tiled=True)  61.9 us
    reduce_scatter x2, waiting for transfers between devices, sum_by_chip(): return lax.psum_scatter(pieces, chips, scatter_dimension=0, tiled=True)[0]  41.2 us
    all_to_all x3, starting transfers between devices, sent_to_all(): lax.all_to_all(jnp.broadcast_to(shard[None], (peers, *shard.shape)), axis...  28.1 us
    reduce_scatter x2, waiting for transfers between devices, sum_by_chip(): pieces = lax.psum_scatter(pieces, core, scatter_dimension=0, tiled=True)  21.7 us
    all_to_all x3, waiting for transfers between devices, sent_to_all(): lax.all_to_all(jnp.broadcast_to(shard[None], (peers, *shard.shape)), axis...  17.3 us
    all_to_all x1, blocking collectives, sent_to_all(): lax.all_to_all(jnp.broadcast_to(shard[None], (peers, *shard.shape)), axis...  13.7 us
    another operation x3, local copies, waits for them, and re-layouts, sum_by_chip(): pieces = pieces.reshape(*sizes, *inside).swapaxes(0, 1).reshape(-1, *inside)  8.41 us
  transfers between devices with their start and end apart: 11, of which 8 were waited for; matrix products, arithmetic and copies ran while one was open for 6% of the time, Pallas kernels for 0%

commit v1 on v0

v1 whole, which is shorter than its diff:
```python
import functools

import jax
import jax.numpy as jnp
from jax import lax
from jax.experimental import pallas as pl
from jax.experimental.pallas import tpu as pltpu
from jax.sharding import PartitionSpec as P

BLK = 128
ROWS = 4
MINE = 4
NBLK = 128
WIDE = 32
F = 256
MESH = pl.DeviceIdType.MESH
BF = jnp.bfloat16
F32 = jnp.float32


def far_first(i):
    return 4 + ((i + 1) // 2) * (1 - 2 * (i % 2))


def nt(a, b):
    return lax.dot_general(a, b, (((1,), (1,)), ((), ())), preferred_element_type=F32)


def kernel(
    cols,
    inv,
    feats_in,
    cot_in,
    w1_cols,
    w2_cols,
    w2_rows,
    vals_in,
    out_ref,
    grads_ref,
    vals,
    feats,
    hid,
    back,
    first,
    v1,
    v2,
    bufs,
    red,
    ssem,
    rvals,
    rcol,
    rgather,
    rred,
    rgrad,
    lsem,
):
    d, c = lax.axis_index("dom"), lax.axis_index("col")
    xlo, z, core = d // 16, (d // 2) % 8, d % 2
    xhi, y = c // 4, c % 4

    def dom_at(xl, zz, cc):
        return (xl * 8 + zz) * 2 + cc

    def col_at(xh, yy):
        return xh * 4 + yy % 4

    up, down = (d, col_at(xhi, y + 1)), (d, col_at(xhi, y + 3))
    across = (d, col_at(1 - xhi, y))
    beside = (dom_at(1 - xlo, z, core), c)
    sibling = (dom_at(xlo, z, 1 - core), c)
    corner = (dom_at(1 - xlo, z, 1 - core), c)

    def along(k):
        return (dom_at(xlo, (z + k) % 8, core), c)

    col_peers = [
        (d, col_at((xhi + a) % 2, y + b)) for a in range(2) for b in range(4) if a + b
    ]

    started = []

    def send(src, dst, sem, to):
        copy = pltpu.make_async_remote_copy(
            src_ref=src,
            dst_ref=dst,
            send_sem=ssem.at[len(started)],
            recv_sem=sem,
            device_id=to,
            device_id_type=MESH,
        )
        copy.start()
        started.append(copy)

    def arrived(dst, sem):
        pltpu.make_async_remote_copy(
            src_ref=dst,
            dst_ref=dst,
            send_sem=ssem.at[0],
            recv_sem=sem,
            device_id=up,
            device_id_type=MESH,
        ).wait_recv()

    barrier = pltpu.get_barrier_semaphore()
    peers = col_peers + [along(k) for k in range(1, 8)] + [beside, sibling, corner]
    for peer in peers:
        pl.semaphore_signal(barrier, inc=1, device_id=peer, device_id_type=MESH)
    pl.semaphore_wait(barrier, len(peers))

    def spread(src, full, which):
        for n, peer in enumerate(col_peers):
            send(src, full.at[c], rcol.at[which, n], peer)

    def collect(full, which):
        for n in range(7):
            arrived(full.at[0], rcol.at[which, n])

    spread(feats_in, feats, 0)

    def part(q, r):
        return vals.at[pl.ds(q * 16 + r * MINE, MINE)]

    own = pltpu.make_async_copy(vals_in, vals.at[pl.ds(c * 16, 16)], lsem)
    own.start()
    for r in range(ROWS):
        src = vals_in.at[pl.ds(r * MINE, MINE)]
        for to in (up, down, across):
            send(src, part(c, r), rvals.at[c, r], to)

    below, above = col_at(xhi, y + 3), col_at(xhi, y + 1)
    partner, opposite = col_at(1 - xhi, y), col_at(xhi, y + 2)
    far_below, far_above = col_at(1 - xhi, y + 3), col_at(1 - xhi, y + 1)
    far_opposite = col_at(1 - xhi, y + 2)

    def take(q, r):
        arrived(part(q, r), rvals.at[q, r])

    def pass_on(q, r, to):
        send(part(q, r), part(q, r), rvals.at[q, r], to)

    def relay(r):
        take(below, r)
        if r < 2:
            pass_on(below, r, up)
        take(above, r)
        if r >= 2:
            pass_on(above, r, down)
        take(partner, r)
        pass_on(partner, r, up)
        pass_on(partner, r, down)

    def cross(r):
        take(opposite, r)
        pass_on(opposite, r, across)

    def at_block(v, xl, zz, cc):
        return v.at[pl.ds(cc * 64 + (xl * 8 + zz) * 4, 4)]

    def gather_start(v, which):
        mine = at_block(v, xlo, z, core)
        for i in range(7):
            send(mine, mine, rgather.at[which, i], along(far_first(i)))
        send(mine, mine, rgather.at[which, 7], beside)

    def gather_relay(v, which):
        for i in range(7):
            zz = (z + 8 - far_first(i)) % 8
            piece = at_block(v, xlo, zz, core)
            arrived(piece, rgather.at[which, i])
            send(piece, piece, rgather.at[which, 8 + i], beside)
        half = v.at[pl.ds(core * 64 + xlo * 32, 32)]
        send(half, half, rgather.at[which, 15], sibling)

    def gather_finish(v, which):
        for i in range(8):
            arrived(at_block(v, 0, 0, 0), rgather.at[which, 7 + i])
        half = v.at[pl.ds(core * 64 + (1 - xlo) * 32, 32)]
        send(half, half, rgather.at[which, 16], sibling)
        arrived(half, rgather.at[which, 15])
        arrived(half, rgather.at[which, 16])

    def put_blocks(v, value):
        base = core * 64 + (xlo * 8 + z) * 4
        for b in range(4):
            v[base + b] = value[:, b * BLK : (b + 1) * BLK].astype(BF)

    def joined(ref):
        return ref[...].reshape(F, ROWS * BLK)

    def product(v):
        def step(q, totals):
            totals = list(totals)
            for r in range(ROWS):
                for s in range(0, MINE, 2):
                    b = q * 16 + r * MINE + s
                    k = q * MINE + s
                    left = jnp.concatenate([v[cols[r, k]], v[cols[r, k + 1]]], axis=1)
                    right = jnp.concatenate([vals[b], vals[b + 1]], axis=1)
                    totals[r] = totals[r] + nt(left, right)
            return tuple(totals)

        zero = jnp.zeros((WIDE, BLK), F32)
        return lax.fori_loop(0, 8, step, (zero,) * ROWS)

    def transposed(g, which):
        to_core, from_core, to_beside, from_beside, to_z, from_z = bufs[6 * which : 6 * which + 6]
        kept = red
        sems = rred.at[which]

        def term(half, xl, i):
            zz = (z + far_first(i)) % 8
            p = dom_at(xl, zz, half) * 4
            sums = []
            for b in range(0, 4, 2):
                total = None
                for r in range(0, ROWS, 2):
                    right = jnp.concatenate(
                        [
                            jnp.concatenate(
                                [vals[inv[r + e, p + b]], vals[inv[r + e, p + b + 1]]], axis=1
                            )
                            for e in range(2)
                        ],
                        axis=0,
                    )
                    got = jnp.dot(
                        g[:, r * BLK : (r + 2) * BLK], right, preferred_element_type=F32
                    )
                    total = got if total is None else total + got
                sums += [total[:, :BLK], total[:, BLK:]]
            return jnp.stack(sums)

        for group in range(4):
            xl = 1 - xlo if group < 2 else xlo

            def one(i, unused):
                to_core[group // 2 * 8 + i] = term(1 - core, xl, i).astype(BF)
                return unused

            at = group % 2 * 4
            lax.fori_loop(at, at + 4, one, 0)
            span = pl.ds(group * 4, 4)
            send(to_core.at[span], from_core.at[span], sems.at[group], sibling)
        for group in range(2):
            span = pl.ds(group * 4, 4)
            arrived(from_core.at[span], sems.at[group])

            def two(i, unused):
                total = term(core, 1 - xlo, i) + from_core[i].astype(F32)
                to_beside[i] = total.astype(BF)
                return unused

            lax.fori_loop(group * 4, group * 4 + 4, two, 0)
            send(to_beside.at[span], from_beside.at[span], sems.at[4 + group], beside)
        for group in range(2):
            arrived(from_core.at[pl.ds(8 + group * 4, 4)], sems.at[2 + group])

            def three(i, unused):
                kept[i] = term(core, xlo, i) + from_core[8 + i].astype(F32)
                return unused

            lax.fori_loop(group * 4, group * 4 + 4, three, 0)
        for group in range(2):
            arrived(from_beside.at[pl.ds(group * 4, 4)], sems.at[4 + group])
            for i in range(group * 4, group * 4 + 4):
                total = kept[i] + from_beside[i].astype(F32)
                if i < 7:
                    to_z[i] = total.astype(BF)
                    send(to_z.at[i], from_z.at[i], sems.at[6 + i], along(far_first(i)))
        for i in range(7):
            arrived(from_z.at[i], sems.at[6 + i])
            total = total + from_z[i].astype(F32)
        return jnp.concatenate([total[b] for b in range(4)], axis=1).astype(BF)

    zero_block = jnp.zeros((1, BLK, BLK), BF)
    vals[pl.ds(NBLK, 1)] = zero_block
    v1[pl.ds(NBLK, 1)] = zero_block[:, :WIDE]
    v2[pl.ds(NBLK, 1)] = zero_block[:, :WIDE]
    feats[c] = feats_in[...]
    collect(feats, 0)
    proj = jnp.dot(w1_cols[...], joined(feats), preferred_element_type=F32)
    put_blocks(v1, proj)
    gather_start(v1, 0)

    relay(0)
    relay(1)
    gather_relay(v1, 0)
    cross(0)
    relay(2)
    cross(1)
    relay(3)
    gather_finish(v1, 0)
    cross(2)
    cross(3)
    for r in range(ROWS):
        for q in (far_below, far_above, far_opposite):
            take(q, r)
    own.wait()

    for r, total in enumerate(product(v1)):
        first[:, r * BLK : (r + 1) * BLK] = total
    hidden = (first[...] * jax.nn.sigmoid(first[...])).astype(BF)
    hid[c] = hidden
    spread(hid.at[c], hid, 1)

    back_second = transposed(cot_in[...], 0)
    back[c] = back_second
    spread(back.at[c], back, 2)

    collect(hid, 1)
    put_blocks(v2, jnp.dot(w2_cols[...], joined(hid), preferred_element_type=F32))
    gather_start(v2, 1)

    collect(back, 2)
    hidden_grad = jnp.dot(w2_rows[...], joined(back), preferred_element_type=F32)
    value = first[...]
    sig = jax.nn.sigmoid(value)
    act_grad = (hidden_grad * (sig + value * sig * (1.0 - sig))).astype(BF)
    back_first = transposed(act_grad, 1)
    grad_second = nt(back[c], joined(hid))
    grad_first = nt(back_first, joined(feats))

    terms, quarters, along_z, whole = bufs[12:16]
    for n, grad in enumerate((grad_second, grad_first)):
        for k in range(4):
            terms[k, n] = grad[k * 8 : k * 8 + 8]
    me = xlo * 2 + core
    pair = [
        (beside, (1 - xlo) * 2 + core),
        (sibling, xlo * 2 + 1 - core),
        (corner, (1 - xlo) * 2 + 1 - core),
    ]
    for n, (to, k) in enumerate(pair):
        send(terms.at[k], quarters.at[n], rgrad.at[n], to)
    gather_relay(v2, 1)
    total = terms[me]
    for n in range(3):
        arrived(quarters.at[n], rgrad.at[n])
        total = total + quarters[n]
    along_z[7] = total
    for i in range(7):
        send(along_z.at[7], along_z.at[i], rgrad.at[3 + i], along(far_first(i)))
    gather_finish(v2, 1)
    for r, total in enumerate(product(v2)):
        out_ref[:, r * BLK : (r + 1) * BLK] = total
    total = along_z[7]
    for i in range(7):
        arrived(along_z.at[i], rgrad.at[3 + i])
        total = total + along_z[i]
    whole[me] = total
    for n, (to, k) in enumerate(pair):
        send(whole.at[me], whole.at[me], rgrad.at[10 + n], to)
    for n, (to, k) in enumerate(pair):
        arrived(whole.at[k], rgrad.at[10 + n])
    for k in range(4):
        for n in range(2):
            grads_ref[n, k * 8 : k * 8 + 8] = whole[k, n]
    for copy in started:
        copy.wait_send()


def body(feats, w_first, w_second, block_cols, block_count, block_vals, cotangent):
    c = lax.axis_index("col")
    slots = jnp.arange(block_cols.shape[1])
    used = slots[None, :] < block_count[:, None]
    b, core, rest = block_cols % 4, block_cols // 4 % 2, block_cols // 8
    cols = jnp.where(used, core * 64 + rest * 4 + b, NBLK).astype(jnp.int32)
    place = slots[None, :] // MINE * 16 + jnp.arange(ROWS)[:, None] * MINE + slots[None, :] % MINE
    hit = used[:, :, None] & (block_cols[:, :, None] == jnp.arange(NBLK)[None, None, :])
    inv = (NBLK + jnp.sum(jnp.where(hit, place[:, :, None] - NBLK, 0), axis=1)).astype(jnp.int32)
    w1_cols = lax.dynamic_slice_in_dim(w_first, c * WIDE, WIDE, 1).T
    w2_cols = lax.dynamic_slice_in_dim(w_second, c * WIDE, WIDE, 1).T
    w2_rows = lax.dynamic_slice_in_dim(w_second, c * WIDE, WIDE, 0)

    blocks = lambda n, kind: pltpu.VMEM((n, 4, WIDE, BLK), kind)
    reduce_bufs = [blocks(16, BF), blocks(16, BF), blocks(8, BF), blocks(8, BF), blocks(8, BF), blocks(8, BF)]
    grad_bufs = [pltpu.VMEM((n, 2, 8, F), F32) for n in (4, 3, 8, 4)]
    vmem = pl.BlockSpec(memory_space=pltpu.VMEM)
    smem = pl.BlockSpec(memory_space=pltpu.SMEM)
    wide = pltpu.VMEM((8, WIDE, ROWS * BLK), BF)
    out, grads = pl.pallas_call(
        kernel,
        out_shape=(
            jax.ShapeDtypeStruct((WIDE, ROWS * BLK), F32),
            jax.ShapeDtypeStruct((2, WIDE, F), F32),
        ),
        in_specs=[smem, smem] + [vmem] * 6,
        out_specs=(vmem, vmem),
        scratch_shapes=[
            pltpu.VMEM((NBLK + 1, BLK, BLK), BF),
            wide,
            wide,
            wide,
            pltpu.VMEM((WIDE, ROWS * BLK), F32),
            pltpu.VMEM((NBLK + 1, WIDE, BLK), BF),
            pltpu.VMEM((NBLK + 1, WIDE, BLK), BF),
            reduce_bufs * 2 + grad_bufs,
            blocks(8, F32),
            pltpu.SemaphoreType.DMA((160,)),
            pltpu.SemaphoreType.DMA((8, 4)),
            pltpu.SemaphoreType.DMA((3, 7)),
            pltpu.SemaphoreType.DMA((2, 17)),
            pltpu.SemaphoreType.DMA((2, 13)),
            pltpu.SemaphoreType.DMA((13,)),
            pltpu.SemaphoreType.DMA,
        ],
        compiler_params=pltpu.CompilerParams(
            collective_id=0, has_side_effects=True, vmem_limit_bytes=40 << 20
        ),
        name="graph_layers",
    )(
        cols,
        inv,
        feats.T,
        cotangent.T,
        w1_cols,
        w2_cols,
        w2_rows,
        block_vals.reshape(ROWS * MINE, BLK, BLK),
    )
    return (out.T, grads[1].T, grads[0].T)


def solution(mesh):
    return jax.shard_map(
        body,
        mesh=mesh,
        in_specs=(
            P("dom", "col"),
            P(),
            P(),
            P("dom", None),
            P("dom"),
            P("dom", "col", None, None),
            P("dom", "col"),
        ),
        out_specs=(P("dom", "col"), P(None, "col"), P(None, "col")),
        check_vma=False,
    )
```

time: 340 us -> 109 us (0.32)
  waiting for transfers between devices: 229 us -> 0 us
  Pallas kernels: 0 us -> 102 us
  starting transfers between devices: 35 us -> 0 us
  matrix products: 22.1 us -> 0 us
  local copies, waits for them, and re-layouts: 21.1 us -> 6.1 us
  between operations: 15.4 us -> 0.68 us
  blocking collectives: 13.7 us -> 0 us
    all_gather x3 -> x0, waiting for transfers between devices: 143 us -> none  [the longest x1 81 us: body(): all_vals = lax.all_gather(block_vals, 'col', axis=1, tiled=True)]
    pallas_call x0 -> x1, Pallas kernels: none -> 102 us  [body(): pl.pallas_call(kernel, out_shape=(jax.ShapeDtypeStruct((WIDE, ROWS * BLK)...]
    reduce_scatter x4 -> x0, waiting for transfers between devices: 62.9 us -> none  [the longest x2 41.2 us: sum_by_chip(): return lax.psum_scatter(pieces, chips, scatter_dimension=0, tiled=True)[0]]
    all_to_all x4 -> x0, starting transfers between devices: 34.5 us -> none  [the longest x3 28.1 us: sent_to_all(): lax.all_to_all(jnp.broadcast_to(shard[None], (peers, *shard.shape)), axis...]
    all_to_all x4 -> x0, waiting for transfers between devices: 22.4 us -> none  [the longest x3 17.3 us: sent_to_all(): lax.all_to_all(jnp.broadcast_to(shard[None], (peers, *shard.shape)), axis...]
    dot_general x11 -> x0, matrix products: 22.1 us -> none  [the longest x2 6.68 us: forward_fold(): jnp.einsum('rkij,rkjf->rif', vals, picked, preferred_element_type=jnp.flo...]
    all_to_all x1 -> x0, blocking collectives: 13.7 us -> none  [sent_to_all(): lax.all_to_all(jnp.broadcast_to(shard[None], (peers, *shard.shape)), axis...]
    another operation x3 -> x0, local copies, waits for them, and re-layouts: 8.41 us -> none  [sum_by_chip(): pieces = pieces.reshape(*sizes, *inside).swapaxes(0, 1).reshape(-1, *inside)]
  transfers between devices with their start and end apart: 11 -> 0, of which waited for: 8 -> 0; matrix products, arithmetic and copies ran while one was open for 6% -> 0% of each run, Pallas kernels for 0% -> 0%
where the time goes in v1:
time: 109 us
  Pallas kernels  102 us (94%)
  local copies, waits for them, and re-layouts  6.1 us (6%)
    pallas_call x1, Pallas kernels, body(): pl.pallas_call(kernel, out_shape=(jax.ShapeDtypeStruct((WIDE, ROWS * BLK)...  102 us
    unnamed x13, local copies, waits for them, and re-layouts  3.78 us

profile of v1, /device:TPU:1, one launch (start us, length us, event | category | flops | bytes accessed | tf_op | source)
XLA Modules:
  0.0 108.8 jit_solution(8153953672755884814)
XLA Ops:
  0.6 0.0 copy-start.4
  0.6 0.6 copy-done.4
  1.3 0.1 iota_compare_fusion.1
  1.4 0.0 copy-start.3
  1.4 0.1 add_add_fusion
  1.4 0.6 copy-done.3
  2.1 0.1 select_reduce_fusion
  2.2 0.1 fusion.5.cols
  2.3 0.7 constant_dynamic-slice_fusion.2.w2_rows
  3.0 1.0 constant_dynamic-slice_fusion
  4.0 0.1 copy.15
  4.0 0.0 copy-start.1
  4.0 0.0 copy-start.2
  4.1 0.1 copy.14
  4.1 0.7 copy-done.1
  4.8 0.0 copy-done.2
  4.8 0.0 copy-start
  4.8 1.0 copy-done
  5.9 101.7 %graph_layers.1 = (f32[32,512]{1,0:T(8,128)S(1)}, f32[2,32,256]{2,1,0:T(8,128)S(1)}) custom-call(s32[4,32]{1,0:T(4,128)S(1)} %fusion.5.cols, s32[4,128]{1,0:T(4,128)S(1)} %broadcast_add_fusion.inv, bf16[32,512]{1,0:T(8,128)(2,1)S(1)} %bitcast.18, bf16[32,512]{1,0:T(8,128)(2,1)S(1)} %bitcast.19, bf16[32,256]{1,0:T(8,128)(2,1)S(1)} %bitcast.16, ...), custom_call_target="tpu_custom_call" | custom-call | tf_op jit(solution)/shard_map/graph_layers/pallas_call | solution.py:381
  107.5 0.6 slice_bitcast_fusion
  108.2 0.6 copy.17
  (3 shorter events, 0.0 us)
Async XLA Ops:
  0.6 0.7 copy-start.4
  1.4 0.7 copy-start.3
  4.0 0.8 copy-start.1
  4.0 0.8 copy-start.2
  4.8 1.0 copy-start

commit v2 on v1

v2 whole, which is shorter than its diff:
```python
import functools

import jax
import jax.numpy as jnp
from jax import lax
from jax.experimental import pallas as pl
from jax.experimental.pallas import tpu as pltpu
from jax.sharding import PartitionSpec as P

BLK = 128
ROWS = 4
MINE = 4
NBLK = 128
WIDE = 32
F = 256
MESH = pl.DeviceIdType.MESH
BF = jnp.bfloat16
F32 = jnp.float32


def far_first(i):
    return 4 + ((i + 1) // 2) * (1 - 2 * (i % 2))


def nt(a, b):
    return lax.dot_general(a, b, (((1,), (1,)), ((), ())), preferred_element_type=F32)


def kernel(
    feats_in,
    cot_in,
    w1_in,
    w2_in,
    vals_in,
    cols_in,
    count_in,
    out_ref,
    grads_ref,
    vals,
    feats,
    hid,
    back,
    first,
    v1,
    v2,
    w1,
    w2,
    w1_t,
    w2_t,
    cot,
    inv_rows,
    cols,
    count,
    inv,
    bufs,
    red,
    ssem,
    rvals,
    rcol,
    rgather,
    rred,
    rgrad,
    lsem,
    news,
):
    d, c = lax.axis_index("dom"), lax.axis_index("col")
    xlo, z, core = d // 16, (d // 2) % 8, d % 2
    xhi, y = c // 4, c % 4

    def dom_at(xl, zz, cc):
        return (xl * 8 + zz) * 2 + cc

    def col_at(xh, yy):
        return xh * 4 + yy % 4

    up, down = (d, col_at(xhi, y + 1)), (d, col_at(xhi, y + 3))
    across = (d, col_at(1 - xhi, y))
    beside = (dom_at(1 - xlo, z, core), c)
    sibling = (dom_at(xlo, z, 1 - core), c)
    corner = (dom_at(1 - xlo, z, 1 - core), c)

    def along(k):
        return (dom_at(xlo, (z + k) % 8, core), c)

    col_peers = [
        (d, col_at((xhi + a) % 2, y + b)) for a in range(2) for b in range(4) if a + b
    ]

    started = []

    def send(src, dst, sem, to):
        copy = pltpu.make_async_remote_copy(
            src_ref=src,
            dst_ref=dst,
            send_sem=ssem.at[len(started)],
            recv_sem=sem,
            device_id=to,
            device_id_type=MESH,
        )
        copy.start()
        started.append(copy)

    def arrived(dst, sem):
        pltpu.make_async_remote_copy(
            src_ref=dst,
            dst_ref=dst,
            send_sem=ssem.at[0],
            recv_sem=sem,
            device_id=up,
            device_id_type=MESH,
        ).wait_recv()

    def local(src, dst, n):
        copy = pltpu.make_async_copy(src, dst, lsem.at[n])
        copy.start()
        return copy

    near = [up, down, across, beside, sibling, corner, along(1), along(7)]
    barrier = pltpu.get_barrier_semaphore()
    for peer in near:
        pl.semaphore_signal(barrier, inc=1, device_id=peer, device_id_type=MESH)
    loads = [
        local(cols_in, cols, 0),
        local(count_in, count, 1),
        local(feats_in, feats.at[c], 2),
        local(w1_in, w1, 3),
        local(w2_in, w2, 4),
        local(cot_in, cot, 5),
        local(vals_in, vals.at[pl.ds(c * 16, 16)], 6),
    ]
    pl.semaphore_wait(barrier, len(near))

    for k in (1, 7):
        pl.semaphore_signal(news.at[0], inc=1, device_id=along(k), device_id_type=MESH)

    def hear_far():
        pl.semaphore_wait(news.at[0], 2)
        for k in (2, 6):
            pl.semaphore_signal(news.at[1], inc=1, device_id=along(k), device_id_type=MESH)

    def spread(src, full, which):
        for n, peer in enumerate(col_peers):
            send(src, full.at[c], rcol.at[which, n], peer)

    def collect(full, which):
        for n in range(7):
            arrived(full.at[0], rcol.at[which, n])

    def part(q, r):
        return feats.at[q] if r == ROWS else vals.at[pl.ds(q * 16 + r * MINE, MINE)]

    def send_own(r, to):
        src = feats_in if r == ROWS else vals_in.at[pl.ds(r * MINE, MINE)]
        send(src, part(c, r), rvals.at[c, r], to)

    for r in (ROWS, 0, 1, 2, 3):
        send_own(r, up)
        send_own((2, 3, 0, 1, ROWS)[r], down)
        send_own(r, across)

    below, above = col_at(xhi, y + 3), col_at(xhi, y + 1)
    partner, opposite = col_at(1 - xhi, y), col_at(xhi, y + 2)
    far_below, far_above = col_at(1 - xhi, y + 3), col_at(1 - xhi, y + 1)
    far_opposite = col_at(1 - xhi, y + 2)

    def take(q, r):
        arrived(part(q, r), rvals.at[q, r])

    def pass_on(q, r, to):
        send(part(q, r), part(q, r), rvals.at[q, r], to)

    def forward(q, r, to):
        take(q, r)
        if to is not None:
            pass_on(q, r, to)

    def both_ways(r):
        take(partner, r)
        pass_on(partner, r, up)
        pass_on(partner, r, down)

    def at_block(v, xl, zz, cc):
        return v.at[pl.ds(cc * 64 + (xl * 8 + zz) * 4, 4)]

    def gather_start(v, which):
        mine = at_block(v, xlo, z, core)
        send(mine, mine, rgather.at[which, 14], beside)
        for i in range(7):
            send(mine, mine, rgather.at[which, i], along(far_first(i)))

    def gather_second(v, which):
        other = at_block(v, 1 - xlo, z, core)
        arrived(other, rgather.at[which, 14])
        for i in range(7):
            send(other, other, rgather.at[which, 7 + i], along(far_first(i)))

    def gather_share(v, which):
        for i in range(14):
            arrived(at_block(v, 0, 0, 0), rgather.at[which, i])
        half = v.at[pl.ds(core * 64, 64)]
        send(half, half, rgather.at[which, 15], sibling)

    def gather_finish(v, which):
        arrived(v.at[pl.ds(0, 64)], rgather.at[which, 15])

    def put_blocks(v, value):
        base = core * 64 + (xlo * 8 + z) * 4
        for b in range(4):
            v[base + b] = value[:, b * BLK : (b + 1) * BLK].astype(BF)

    def joined(ref):
        return ref[...].reshape(F, ROWS * BLK)

    def block_of(r, k):
        p = cols[r, k]
        return jnp.where(k < count[r], p // 4 % 2 * 64 + p // 8 * 4 + p % 4, NBLK)

    def product(v, rows):
        def step(q, totals):
            totals = list(totals)
            for n, r in enumerate(rows):
                for s in range(0, MINE, 2):
                    b = q * 16 + r * MINE + s
                    k = q * MINE + s
                    left = jnp.concatenate([v[block_of(r, k)], v[block_of(r, k + 1)]], axis=1)
                    right = jnp.concatenate([vals[b], vals[b + 1]], axis=1)
                    totals[n] = totals[n] + nt(left, right)
            return tuple(totals)

        zero = jnp.zeros((WIDE, BLK), F32)
        return lax.fori_loop(0, 8, step, (zero,) * len(rows), unroll=4)

    def transposed(g, which, meanwhile):
        to_core, from_core, to_beside, from_beside, to_z, from_z = bufs[6 * which : 6 * which + 6]
        kept = red
        sems = rred.at[which]

        def term(half, xl, i):
            zz = (z + far_first(i)) % 8
            p = dom_at(xl, zz, half) * 4
            sums = []
            for b in range(0, 4, 2):
                total = None
                for r in range(0, ROWS, 2):
                    right = jnp.concatenate(
                        [
                            jnp.concatenate(
                                [vals[inv[r + e, p + b]], vals[inv[r + e, p + b + 1]]], axis=1
                            )
                            for e in range(2)
                        ],
                        axis=0,
                    )
                    got = jnp.dot(
                        g[:, r * BLK : (r + 2) * BLK], right, preferred_element_type=F32
                    )
                    total = got if total is None else total + got
                sums += [total[:, :BLK], total[:, BLK:]]
            return jnp.stack(sums)

        def over(at, n, write):
            def one(i, unused):
                write(i)
                return unused

            lax.fori_loop(at, at + n, one, 0, unroll=n)

        for group in range(4):
            xl = 1 - xlo if group < 2 else xlo

            def one(i):
                to_core[group // 2 * 8 + i] = term(1 - core, xl, i).astype(BF)

            over(group % 2 * 4, 4, one)
            span = pl.ds(group * 4, 4)
            send(to_core.at[span], from_core.at[span], sems.at[group], sibling)
        for group in range(4):
            if group % 2 == 0:
                arrived(from_core.at[pl.ds(group * 2, 4)], sems.at[group // 2])

            def two(i):
                total = term(core, 1 - xlo, i) + from_core[i].astype(F32)
                to_beside[i] = total.astype(BF)

            over(group * 2, 2, two)
            span = pl.ds(group * 2, 2)
            send(to_beside.at[span], from_beside.at[span], sems.at[4 + group], beside)
        for group in range(2):
            arrived(from_core.at[pl.ds(8 + group * 4, 4)], sems.at[2 + group])

            def three(i):
                kept[i] = term(core, xlo, i) + from_core[8 + i].astype(F32)

            over(group * 4, 4, three)
        meanwhile[0]()
        for group in range(4):
            arrived(from_beside.at[pl.ds(group * 2, 2)], sems.at[4 + group])
            for i in range(group * 2, group * 2 + 2):
                total = kept[i] + from_beside[i].astype(F32)
                if i < 7:
                    to_z[i] = total.astype(BF)
                    send(to_z.at[i], from_z.at[i], sems.at[8 + i], along(far_first(i)))
        kept[7] = total
        meanwhile[1]()
        total = kept[7]
        for i in range(7):
            arrived(from_z.at[i], sems.at[8 + i])
            total = total + from_z[i].astype(F32)
        return jnp.concatenate([total[b] for b in range(4)], axis=1).astype(BF)

    zero_block = jnp.zeros((1, BLK, BLK), BF)
    vals[pl.ds(NBLK, 1)] = zero_block
    v1[pl.ds(NBLK, 1)] = zero_block[:, :WIDE]
    v2[pl.ds(NBLK, 1)] = zero_block[:, :WIDE]
    hear_far()
    for copy in loads:
        copy.wait()
    lane = lax.broadcasted_iota(jnp.int32, (1, NBLK), 1)
    for r in range(ROWS):

        def mark(k, found):
            place = k // MINE * 16 + r * MINE + k % MINE - NBLK
            return found + jnp.where((lane == cols[r, k]) & (k < count[r]), place, 0)

        empty = jnp.full((1, NBLK), NBLK, jnp.int32)
        inv_rows[r : r + 1] = lax.fori_loop(0, 32, mark, empty, unroll=8)
    to_scalars = local(inv_rows, inv, 0)
    forward(below, ROWS, up)
    forward(above, ROWS, None)
    both_ways(ROWS)
    w1_t[...] = w1[...].T
    forward(below, 0, up)
    forward(above, 2, down)
    w2_t[...] = w2[...].T
    forward(opposite, ROWS, across)
    for q in (far_below, far_above, far_opposite):
        take(q, ROWS)
    pl.semaphore_wait(news.at[1], 2)
    mine = pl.ds(c * WIDE, WIDE)
    put_blocks(v1, jnp.dot(w1_t[mine, :], joined(feats), preferred_element_type=F32))
    gather_start(v1, 0)

    both_ways(0)
    forward(below, 1, up)
    forward(above, 3, down)
    forward(opposite, 0, across)
    forward(opposite, 2, across)
    gather_second(v1, 0)
    both_ways(1)
    forward(opposite, 1, across)
    forward(opposite, 3, across)
    both_ways(2)
    both_ways(3)
    gather_share(v1, 0)
    for q, rows in ((below, (2, 3)), (above, (0, 1))):
        for r in rows:
            take(q, r)
    to_scalars.wait()
    for r in range(ROWS):
        for q in (far_below, far_above, far_opposite):
            take(q, r)
    gather_finish(v1, 0)

    def layer_rows(rows):
        for r, total in zip(rows, product(v1, rows)):
            first[:, r * BLK : (r + 1) * BLK] = total

    def after_first():
        layer_rows((2, 3))
        hidden = (first[...] * jax.nn.sigmoid(first[...])).astype(BF)
        hid[c] = hidden
        spread(hid.at[c], hid, 1)

    back_second = transposed(cot[...], 0, (lambda: layer_rows((0, 1)), after_first))
    back[c] = back_second
    spread(back.at[c], back, 2)

    collect(hid, 1)
    put_blocks(v2, jnp.dot(w2_t[mine, :], joined(hid), preferred_element_type=F32))
    gather_start(v2, 1)
    gather_second(v2, 1)

    collect(back, 2)
    hidden_grad = jnp.dot(w2[mine, :], joined(back), preferred_element_type=F32)
    value = first[...]
    sig = jax.nn.sigmoid(value)
    act_grad = (hidden_grad * (sig + value * sig * (1.0 - sig))).astype(BF)
    back_first = transposed(
        act_grad, 1, (lambda: None, lambda: gather_share(v2, 1))
    )
    grad_second = nt(back[c], joined(hid))
    grad_first = nt(back_first, joined(feats))

    terms, quarters, along_z, whole = bufs[12:16]
    for n, grad in enumerate((grad_second, grad_first)):
        for k in range(4):
            terms[k, n] = grad[k * 8 : k * 8 + 8]
    me = xlo * 2 + core
    pair = [
        (beside, (1 - xlo) * 2 + core),
        (sibling, xlo * 2 + 1 - core),
        (corner, (1 - xlo) * 2 + 1 - core),
    ]
    for n, (to, k) in enumerate(pair):
        send(terms.at[k], quarters.at[n], rgrad.at[n], to)
    total = terms[me]
    for n in range(3):
        arrived(quarters.at[n], rgrad.at[n])
        total = total + quarters[n]
    along_z[7] = total
    for i in range(7):
        send(along_z.at[7], along_z.at[i], rgrad.at[3 + i], along(far_first(i)))
    gather_finish(v2, 1)
    for r, total in enumerate(product(v2, range(ROWS))):
        out_ref[:, r * BLK : (r + 1) * BLK] = total
    total = along_z[7]
    for i in range(7):
        arrived(along_z.at[i], rgrad.at[3 + i])
        total = total + along_z[i]
    whole[me] = total
    for n, (to, k) in enumerate(pair):
        send(whole.at[me], whole.at[me], rgrad.at[10 + n], to)
    for n, (to, k) in enumerate(pair):
        arrived(whole.at[k], rgrad.at[10 + n])
    for k in range(4):
        for n in range(2):
            grads_ref[n, k * 8 : k * 8 + 8] = whole[k, n]
    for copy in started:
        copy.wait_send()


def body(feats, w_first, w_second, block_cols, block_count, block_vals, cotangent):
    def blocks(n, kind):
        return pltpu.VMEM((n, 4, WIDE, BLK), kind)

    reduce_bufs = [blocks(n, BF) for n in (16, 16, 8, 8, 8, 8)]
    grad_bufs = [pltpu.VMEM((n, 2, 8, F), F32) for n in (4, 3, 8, 4)]
    vmem = pl.BlockSpec(memory_space=pltpu.VMEM)
    anywhere = pl.BlockSpec(memory_space=pl.ANY)
    wide = pltpu.VMEM((8, WIDE, ROWS * BLK), BF)
    square = pltpu.VMEM((F, F), BF)
    dma = pltpu.SemaphoreType.DMA
    out, grads = pl.pallas_call(
        kernel,
        out_shape=(
            jax.ShapeDtypeStruct((WIDE, ROWS * BLK), F32),
            jax.ShapeDtypeStruct((2, WIDE, F), F32),
        ),
        in_specs=[anywhere] * 7,
        out_specs=(vmem, vmem),
        scratch_shapes=[
            pltpu.VMEM((NBLK + 1, BLK, BLK), BF),
            wide,
            wide,
            wide,
            pltpu.VMEM((WIDE, ROWS * BLK), F32),
            pltpu.VMEM((NBLK + 1, WIDE, BLK), BF),
            pltpu.VMEM((NBLK + 1, WIDE, BLK), BF),
            square,
            square,
            square,
            square,
            pltpu.VMEM((WIDE, ROWS * BLK), BF),
            pltpu.VMEM((ROWS, NBLK), jnp.int32),
            pltpu.SMEM((ROWS, 32), jnp.int32),
            pltpu.SMEM((ROWS,), jnp.int32),
            pltpu.SMEM((ROWS, NBLK), jnp.int32),
            reduce_bufs * 2 + grad_bufs,
            blocks(8, F32),
            dma((160,)),
            dma((8, 5)),
            dma((3, 7)),
            dma((2, 16)),
            dma((2, 15)),
            dma((13,)),
            dma((7,)),
            pltpu.SemaphoreType.REGULAR((2,)),
        ],
        compiler_params=pltpu.CompilerParams(
            collective_id=0, has_side_effects=True, vmem_limit_bytes=56 << 20
        ),
        name="graph_layers",
    )(
        feats.T,
        cotangent.T,
        w_first,
        w_second,
        block_vals.reshape(ROWS * MINE, BLK, BLK),
        block_cols,
        block_count,
    )
    return (out.T, grads[1].T, grads[0].T)


def solution(mesh):
    return jax.shard_map(
        body,
        mesh=mesh,
        in_specs=(
            P("dom", "col"),
            P(),
            P(),
            P("dom", None),
            P("dom"),
            P("dom", "col", None, None),
            P("dom", "col"),
        ),
        out_specs=(P("dom", "col"), P(None, "col"), P(None, "col")),
        check_vma=False,
    )
```

time: 109 us -> 96.3 us (0.88)
  Pallas kernels: 102 us -> 93.5 us
  local copies, waits for them, and re-layouts: 6.1 us -> 2.07 us
    pallas_call x1, Pallas kernels: 102 us -> 93.5 us  [body(): pl.pallas_call(kernel, out_shape=(jax.ShapeDtypeStruct((WIDE, ROWS * BLK)...]
    unnamed x13 -> x3, local copies, waits for them, and re-layouts: 3.78 us -> 0.63 us
    dynamic_slice x2 -> x0, local copies, waits for them, and re-layouts: 1.69 us -> none  [the longest x1 0.97 us: body(): w2_cols = lax.dynamic_slice_in_dim(w_second, c * WIDE, WIDE, 1).T]
where the time goes in v2:
time: 96.3 us; the launch traced here: 96.2 us
  Pallas kernels  93.5 us (97%)
  local copies, waits for them, and re-layouts  2.07 us (2%)
    pallas_call x1, Pallas kernels, body(): pl.pallas_call(kernel, out_shape=(jax.ShapeDtypeStruct((WIDE, ROWS * BLK)...  93.5 us

profile of v2, /device:TPU:1, one launch (start us, length us, event | category | flops | bytes accessed | tf_op | source)
XLA Modules:
  0.0 96.2 jit_solution(3127079805470565442)
XLA Ops:
  0.6 93.5 %graph_layers.1 = (f32[32,512]{1,0:T(8,128)}, f32[2,32,256]{2,1,0:T(8,128)}) custom-call(bf16[32,512]{1,0:T(8,128)(2,1)} %bitcast.14, bf16[32,512]{1,0:T(8,128)(2,1)} %bitcast.15, bf16[256,256]{1,0:T(8,128)(2,1)} %w1_in.1, bf16[256,256]{1,0:T(8,128)(2,1)} %w2_in.1, bf16[16,128,128]{2,1,0:T(8,128)(2,1)} %bitcast.12, s32[4,32]{1,0:T(4,128)} %cols_in.1, s32[4]{0:T(128)} %count_in.1), custom_call_target="tpu_custom_call" | custom-call | tf_op jit(solution)/shard_map/graph_layers/pallas_call | solution.py:443
  94.1 0.0 copy-start
  94.1 1.4 %slice_bitcast_fusion = (f32[256,32]{0,1:T(8,128)}, f32[256,32]{0,1:T(8,128)}) fusion(f32[2,32,256]{2,1,0:T(8,128)} %get-tuple-element.6), kind=kLoop, calls=%fused_computation | loop fusion | bytes 131072 | tf_op jit(solution)/shard_map/transpose | solution.py:492
  95.6 0.0 copy-done
  95.6 0.6 copy.11
Async XLA Ops:
  94.1 1.4 %copy-start = (f32[32,512]{1,0:T(8,128)S(1)}, f32[32,512]{1,0:T(8,128)}, u32[]{:S(2)}) copy-start(f32[32,512]{1,0:T(8,128)} %get-tuple-element.5) | copy-start | bytes 196612

commit v3 on v2

--- a/solution.py
+++ b/solution.py
@@ -38,6 +38,7 @@
     grads_ref,
     vals,
     feats,
+    agg,
     hid,
     back,
     first,
@@ -53,7 +54,7 @@
     count,
     inv,
     bufs,
-    red,
+    gbufs,
     ssem,
     rvals,
     rcol,
@@ -122,9 +123,9 @@
     loads = [
         local(cols_in, cols, 0),
         local(count_in, count, 1),
-        local(feats_in, feats.at[c], 2),
         local(w1_in, w1, 3),
         local(w2_in, w2, 4),
+        local(feats_in, feats, 2),
         local(cot_in, cot, 5),
         local(vals_in, vals.at[pl.ds(c * 16, 16)], 6),
     ]
@@ -147,15 +148,14 @@
             arrived(full.at[0], rcol.at[which, n])
 
     def part(q, r):
-        return feats.at[q] if r == ROWS else vals.at[pl.ds(q * 16 + r * MINE, MINE)]
+        return vals.at[pl.ds(q * 16 + r * MINE, MINE)]
 
     def send_own(r, to):
-        src = feats_in if r == ROWS else vals_in.at[pl.ds(r * MINE, MINE)]
-        send(src, part(c, r), rvals.at[c, r], to)
-
-    for r in (ROWS, 0, 1, 2, 3):
+        send(vals_in.at[pl.ds(r * MINE, MINE)], part(c, r), rvals.at[c, r], to)
+
+    for r in range(ROWS):
         send_own(r, up)
-        send_own((2, 3, 0, 1, ROWS)[r], down)
+        send_own((2, 3, 0, 1)[r], down)
         send_own(r, across)
 
     below, above = col_at(xhi, y + 3), col_at(xhi, y + 1)
@@ -230,10 +230,9 @@
         zero = jnp.zeros((WIDE, BLK), F32)
         return lax.fori_loop(0, 8, step, (zero,) * len(rows), unroll=4)
 
-    def transposed(g, which, meanwhile):
-        to_core, from_core, to_beside, from_beside, to_z, from_z = bufs[6 * which : 6 * which + 6]
-        kept = red
-        sems = rred.at[which]
+    def transposed(g, meanwhile):
+        to_core, from_core, to_beside, from_beside, to_z, from_z, kept = bufs
+        sems = rred
 
         def term(half, xl, i):
             zz = (z + far_first(i)) % 8
@@ -315,6 +314,9 @@
     hear_far()
     for copy in loads:
         copy.wait()
+    put_blocks(v1, feats[...])
+    pl.semaphore_wait(news.at[1], 2)
+    gather_start(v1, 0)
     lane = lax.broadcasted_iota(jnp.int32, (1, NBLK), 1)
     for r in range(ROWS):
 
@@ -325,33 +327,22 @@
         empty = jnp.full((1, NBLK), NBLK, jnp.int32)
         inv_rows[r : r + 1] = lax.fori_loop(0, 32, mark, empty, unroll=8)
     to_scalars = local(inv_rows, inv, 0)
-    forward(below, ROWS, up)
-    forward(above, ROWS, None)
-    both_ways(ROWS)
-    w1_t[...] = w1[...].T
     forward(below, 0, up)
     forward(above, 2, down)
-    w2_t[...] = w2[...].T
-    forward(opposite, ROWS, across)
-    for q in (far_below, far_above, far_opposite):
-        take(q, ROWS)
-    pl.semaphore_wait(news.at[1], 2)
-    mine = pl.ds(c * WIDE, WIDE)
-    put_blocks(v1, jnp.dot(w1_t[mine, :], joined(feats), preferred_element_type=F32))
-    gather_start(v1, 0)
-
+    gather_second(v1, 0)
     both_ways(0)
     forward(below, 1, up)
     forward(above, 3, down)
     forward(opposite, 0, across)
     forward(opposite, 2, across)
-    gather_second(v1, 0)
+    w1_t[...] = w1[...].T
+    w2_t[...] = w2[...].T
     both_ways(1)
     forward(opposite, 1, across)
     forward(opposite, 3, across)
     both_ways(2)
+    gather_share(v1, 0)
     both_ways(3)
-    gather_share(v1, 0)
     for q, rows in ((below, (2, 3)), (above, (0, 1))):
         for r in rows:
             take(q, r)
@@ -361,70 +352,86 @@
             take(q, r)
     gather_finish(v1, 0)
 
-    def layer_rows(rows):
-        for r, total in zip(rows, product(v1, rows)):
-            first[:, r * BLK : (r + 1) * BLK] = total
-
-    def after_first():
-        layer_rows((2, 3))
-        hidden = (first[...] * jax.nn.sigmoid(first[...])).astype(BF)
-        hid[c] = hidden
+    for r, total in enumerate(product(v1, range(ROWS))):
+        agg[c, :, r * BLK : (r + 1) * BLK] = total.astype(BF)
+    spread(agg.at[c], agg, 0)
+    mine = pl.ds(c * WIDE, WIDE)
+
+    def after_agg():
+        collect(agg, 0)
+        value = jnp.dot(w1_t[mine, :], joined(agg), preferred_element_type=F32)
+        first[...] = value
+        hid[c] = (value * jax.nn.sigmoid(value)).astype(BF)
         spread(hid.at[c], hid, 1)
 
-    back_second = transposed(cot[...], 0, (lambda: layer_rows((0, 1)), after_first))
-    back[c] = back_second
+    def after_hidden():
+        collect(hid, 1)
+        put_blocks(v2, jnp.dot(w2_t[mine, :], joined(hid), preferred_element_type=F32))
+        gather_start(v2, 1)
+
+    back[c] = transposed(cot[...], (after_agg, after_hidden))
     spread(back.at[c], back, 2)
-
-    collect(hid, 1)
-    put_blocks(v2, jnp.dot(w2_t[mine, :], joined(hid), preferred_element_type=F32))
-    gather_start(v2, 1)
     gather_second(v2, 1)
 
-    collect(back, 2)
-    hidden_grad = jnp.dot(w2[mine, :], joined(back), preferred_element_type=F32)
-    value = first[...]
-    sig = jax.nn.sigmoid(value)
-    act_grad = (hidden_grad * (sig + value * sig * (1.0 - sig))).astype(BF)
-    back_first = transposed(
-        act_grad, 1, (lambda: None, lambda: gather_share(v2, 1))
-    )
-    grad_second = nt(back[c], joined(hid))
-    grad_first = nt(back_first, joined(feats))
-
-    terms, quarters, along_z, whole = bufs[12:16]
-    for n, grad in enumerate((grad_second, grad_first)):
-        for k in range(4):
-            terms[k, n] = grad[k * 8 : k * 8 + 8]
     me = xlo * 2 + core
     pair = [
         (beside, (1 - xlo) * 2 + core),
         (sibling, xlo * 2 + 1 - core),
         (corner, (1 - xlo) * 2 + 1 - core),
     ]
-    for n, (to, k) in enumerate(pair):
-        send(terms.at[k], quarters.at[n], rgrad.at[n], to)
-    total = terms[me]
-    for n in range(3):
-        arrived(quarters.at[n], rgrad.at[n])
-        total = total + quarters[n]
-    along_z[7] = total
-    for i in range(7):
-        send(along_z.at[7], along_z.at[i], rgrad.at[3 + i], along(far_first(i)))
+
+    def quarters_out(n, grad):
+        terms, quarters, along_z, whole = gbufs[n]
+        for k in range(4):
+            terms[k] = grad[k * 8 : k * 8 + 8]
+        for i, (to, k) in enumerate(pair):
+            send(terms.at[k], quarters.at[i], rgrad.at[n, i], to)
+
+    def sums_out(n):
+        terms, quarters, along_z, whole = gbufs[n]
+        total = terms[me]
+        for i in range(3):
+            arrived(quarters.at[i], rgrad.at[n, i])
+            total = total + quarters[i]
+        along_z[7] = total
+        for i in range(7):
+            send(along_z.at[7], along_z.at[i], rgrad.at[n, 3 + i], along(far_first(i)))
+
+    def totals_out(n):
+        terms, quarters, along_z, whole = gbufs[n]
+        total = along_z[7]
+        for i in range(7):
+            arrived(along_z.at[i], rgrad.at[n, 3 + i])
+            total = total + along_z[i]
+        whole[me] = total
+        for i, (to, k) in enumerate(pair):
+            send(whole.at[me], whole.at[me], rgrad.at[n, 10 + i], to)
+
+    def totals_in(n):
+        terms, quarters, along_z, whole = gbufs[n]
+        for i, (to, k) in enumerate(pair):
+            arrived(whole.at[k], rgrad.at[n, 10 + i])
+        for k in range(4):
+            grads_ref[n, k * 8 : k * 8 + 8] = whole[k]
+
+    quarters_out(0, nt(back[c], joined(hid)))
+    collect(back, 2)
+    hidden_grad = jnp.dot(w2[mine, :], joined(back), preferred_element_type=F32)
+    value = first[...]
+    sig = jax.nn.sigmoid(value)
+    act_grad = (hidden_grad * (sig + value * sig * (1.0 - sig))).astype(BF)
+    quarters_out(1, nt(act_grad, joined(agg)))
+    sums_out(0)
+    sums_out(1)
+    gather_share(v2, 1)
+    totals_out(0)
+    totals_out(1)
+
     gather_finish(v2, 1)
     for r, total in enumerate(product(v2, range(ROWS))):
         out_ref[:, r * BLK : (r + 1) * BLK] = total
-    total = along_z[7]
-    for i in range(7):
-        arrived(along_z.at[i], rgrad.at[3 + i])
-        total = total + along_z[i]
-    whole[me] = total
-    for n, (to, k) in enumerate(pair):
-        send(whole.at[me], whole.at[me], rgrad.at[10 + n], to)
-    for n, (to, k) in enumerate(pair):
-        arrived(whole.at[k], rgrad.at[10 + n])
-    for k in range(4):
-        for n in range(2):
-            grads_ref[n, k * 8 : k * 8 + 8] = whole[k, n]
+    totals_in(0)
+    totals_in(1)
     for copy in started:
         copy.wait_send()
 
@@ -434,7 +441,7 @@
         return pltpu.VMEM((n, 4, WIDE, BLK), kind)
 
     reduce_bufs = [blocks(n, BF) for n in (16, 16, 8, 8, 8, 8)]
-    grad_bufs = [pltpu.VMEM((n, 2, 8, F), F32) for n in (4, 3, 8, 4)]
+    grad_bufs = [[pltpu.VMEM((n, 8, F), F32) for n in (4, 3, 8, 4)] for unused in range(2)]
     vmem = pl.BlockSpec(memory_space=pltpu.VMEM)
     anywhere = pl.BlockSpec(memory_space=pl.ANY)
     wide = pltpu.VMEM((8, WIDE, ROWS * BLK), BF)
@@ -450,6 +457,7 @@
         out_specs=(vmem, vmem),
         scratch_shapes=[
             pltpu.VMEM((NBLK + 1, BLK, BLK), BF),
+            pltpu.VMEM((WIDE, ROWS * BLK), BF),
             wide,
             wide,
             wide,
@@ -465,14 +473,14 @@
             pltpu.SMEM((ROWS, 32), jnp.int32),
             pltpu.SMEM((ROWS,), jnp.int32),
             pltpu.SMEM((ROWS, NBLK), jnp.int32),
-            reduce_bufs * 2 + grad_bufs,
-            blocks(8, F32),
+            reduce_bufs + [blocks(8, F32)],
+            grad_bufs,
             dma((160,)),
-            dma((8, 5)),
+            dma((8, 4)),
             dma((3, 7)),
             dma((2, 16)),
-            dma((2, 15)),
-            dma((13,)),
+            dma((15,)),
+            dma((2, 13)),
             dma((7,)),
             pltpu.SemaphoreType.REGULAR((2,)),
         ],

time: 96.3 us -> 80.6 us (0.84)
  Pallas kernels: 93.5 us -> 77.7 us
    pallas_call x1, Pallas kernels: 93.5 us -> 77.7 us  [body(): pl.pallas_call(kernel, out_shape=(jax.ShapeDtypeStruct((WIDE, ROWS * BLK)...]
where the time goes in v3:
time: 80.6 us; the launch traced here: 80.5 us
  Pallas kernels  77.7 us (96%)
  local copies, waits for them, and re-layouts  2.07 us (3%)
    pallas_call x1, Pallas kernels, body(): pl.pallas_call(kernel, out_shape=(jax.ShapeDtypeStruct((WIDE, ROWS * BLK)...  77.7 us

profile of v3, /device:TPU:1, one launch (start us, length us, event | category | flops | bytes accessed | tf_op | source)
XLA Modules:
  0.0 80.5 jit_solution(5382362392257202287)
XLA Ops:
  0.6 77.7 %graph_layers.1 = (f32[32,512]{1,0:T(8,128)}, f32[2,32,256]{2,1,0:T(8,128)}) custom-call(bf16[32,512]{1,0:T(8,128)(2,1)} %bitcast.14, bf16[32,512]{1,0:T(8,128)(2,1)} %bitcast.15, bf16[256,256]{1,0:T(8,128)(2,1)} %w1_in.1, bf16[256,256]{1,0:T(8,128)(2,1)} %w2_in.1, bf16[16,128,128]{2,1,0:T(8,128)(2,1)} %bitcast.12, s32[4,32]{1,0:T(4,128)} %cols_in.1, s32[4]{0:T(128)} %count_in.1), custom_call_target="tpu_custom_call" | custom-call | tf_op jit(solution)/shard_map/graph_layers/pallas_call | solution.py:450
  78.4 0.0 copy-start
  78.4 1.4 %slice_bitcast_fusion = (f32[256,32]{0,1:T(8,128)}, f32[256,32]{0,1:T(8,128)}) fusion(f32[2,32,256]{2,1,0:T(8,128)} %get-tuple-element.6), kind=kLoop, calls=%fused_computation | loop fusion | bytes 131072 | tf_op jit(solution)/shard_map/transpose | solution.py:500
  79.8 0.0 copy-done
  79.8 0.6 copy.11
Async XLA Ops:
  78.4 1.4 %copy-start = (f32[32,512]{1,0:T(8,128)S(1)}, f32[32,512]{1,0:T(8,128)}, u32[]{:S(2)}) copy-start(f32[32,512]{1,0:T(8,128)} %get-tuple-element.5) | copy-start | bytes 196612

commit v4 on v3

v4 whole, which is shorter than its diff:
```python
import functools

import jax
import jax.numpy as jnp
from jax import lax
from jax.experimental import pallas as pl
from jax.experimental.pallas import tpu as pltpu
from jax.sharding import PartitionSpec as P

BLK = 128
ROWS = 4
MINE = 4
NBLK = 128
MEANWHILE = 4
WIDE = 32
F = 256
MESH = pl.DeviceIdType.MESH
BF = jnp.bfloat16
F32 = jnp.float32


def far_first(i):
    return 4 + ((i + 1) // 2) * (1 - 2 * (i % 2))


def nt(a, b):
    return lax.dot_general(a, b, (((1,), (1,)), ((), ())), preferred_element_type=F32)


def kernel(
    feats_in,
    cot_in,
    w1_in,
    w2_in,
    vals_in,
    cols_in,
    count_in,
    out_ref,
    grads_ref,
    vals,
    feats,
    agg,
    hid,
    back,
    first,
    v1,
    v2,
    w1,
    w2,
    w1_t,
    w2_t,
    cot,
    inv_rows,
    cols,
    count,
    inv,
    bufs,
    gbufs,
    ssem,
    rvals,
    rcol,
    rgather,
    rred,
    rgrad,
    lsem,
    rhalf,
    news,
):
    d, c = lax.axis_index("dom"), lax.axis_index("col")
    xlo, z, core = d // 16, (d // 2) % 8, d % 2
    xhi, y = c // 4, c % 4

    def dom_at(xl, zz, cc):
        return (xl * 8 + zz) * 2 + cc

    def col_at(xh, yy):
        return xh * 4 + yy % 4

    up, down = (d, col_at(xhi, y + 1)), (d, col_at(xhi, y + 3))
    across = (d, col_at(1 - xhi, y))
    beside = (dom_at(1 - xlo, z, core), c)
    sibling = (dom_at(xlo, z, 1 - core), c)
    corner = (dom_at(1 - xlo, z, 1 - core), c)

    def along(k):
        return (dom_at(xlo, (z + k) % 8, core), c)

    col_peers = [
        (d, col_at((xhi + a) % 2, y + b)) for a in range(2) for b in range(4) if a + b
    ]

    def send(src, dst, sem, to, group):
        pltpu.make_async_remote_copy(
            src_ref=src,
            dst_ref=dst,
            send_sem=ssem.at[group],
            recv_sem=sem,
            device_id=to,
            device_id_type=MESH,
        ).start()

    def sent(ref, group):
        pltpu.make_async_remote_copy(
            src_ref=ref,
            dst_ref=ref,
            send_sem=ssem.at[group],
            recv_sem=rhalf.at[0],
            device_id=up,
            device_id_type=MESH,
        ).wait_send()

    def arrived(dst, sem):
        pltpu.make_async_remote_copy(
            src_ref=dst,
            dst_ref=dst,
            send_sem=ssem.at[0],
            recv_sem=sem,
            device_id=up,
            device_id_type=MESH,
        ).wait_recv()

    def local(src, dst, n):
        copy = pltpu.make_async_copy(src, dst, lsem.at[n])
        copy.start()
        return copy

    near = [up, down, across, beside, sibling, corner, along(1), along(7)]
    barrier = pltpu.get_barrier_semaphore()
    for peer in near:
        pl.semaphore_signal(barrier, inc=1, device_id=peer, device_id_type=MESH)
    loads = [
        local(cols_in, cols, 0),
        local(count_in, count, 1),
        local(w1_in, w1, 7),
        local(w2_in, w2, 4),
        local(feats_in, feats, 2),
        local(cot_in, cot, 5),
        local(vals_in.at[pl.ds(0, 8)], vals[0].at[pl.ds(c * 8, 8)], 6),
        local(vals_in.at[pl.ds(8, 8)], vals[1].at[pl.ds(c * 8, 8)], 3),
    ]
    pl.semaphore_wait(barrier, len(near))

    for k in (1, 7):
        pl.semaphore_signal(news.at[0], inc=1, device_id=along(k), device_id_type=MESH)

    def hear_far():
        pl.semaphore_wait(news.at[0], 2)
        for k in (2, 6):
            pl.semaphore_signal(news.at[1], inc=1, device_id=along(k), device_id_type=MESH)

    def spread(src, full, which):
        for peer in col_peers:
            send(src, full.at[c], rcol.at[which], peer, 3 + which)

    def collect(full, which):
        arrived(full.at[pl.ds(0, 7)], rcol.at[which])

    def part(q, r):
        return vals[r // 2].at[pl.ds(q * 8 + r % 2 * MINE, MINE)]

    def second_half(q):
        return vals[1].at[pl.ds(q * 8 + MINE + 2, 2)]

    def send_own(r, to):
        send(vals_in.at[pl.ds(r * MINE, MINE)], part(c, r), rvals.at[c, r], to, 0)

    for r in range(ROWS):
        send_own(r, up)
        send_own((2, 3, 0, 1)[r], down)
        send_own(r, across)

    below, above = col_at(xhi, y + 3), col_at(xhi, y + 1)
    partner, opposite = col_at(1 - xhi, y), col_at(xhi, y + 2)
    far_below, far_above = col_at(1 - xhi, y + 3), col_at(1 - xhi, y + 1)
    far_opposite = col_at(1 - xhi, y + 2)

    def take(q, r):
        arrived(part(q, r), rvals.at[q, r])

    def pass_on(q, r, to):
        send(part(q, r), part(q, r), rvals.at[q, r], to, 1)

    def forward(q, r, to):
        take(q, r)
        if to is not None:
            pass_on(q, r, to)

    def both_ways(r):
        take(partner, r)
        piece = part(partner, r)
        send(piece, piece, rvals.at[partner, r], up, 1)
        send(piece, piece, rvals.at[partner, r], down, 1)

    def at_block(v, xl, zz, cc):
        return v.at[pl.ds(cc * 64 + (xl * 8 + zz) * 4, 4)]

    def gather_start(v, which, far):
        mine = at_block(v, xlo, z, core)
        send(mine, mine, rgather.at[which, 0], beside, 2 + 4 * which)
        for i in range(7):
            sem = rgather.at[which, 2 if i >= far else 4 + i]
            send(mine, mine, sem, along(far_first(i)), 2 + 4 * which)

    def gather_second(v, which, far):
        other = at_block(v, 1 - xlo, z, core)
        arrived(other, rgather.at[which, 0])
        for i in range(far, 7):
            send(other, other, rgather.at[which, 3], along(far_first(i)), 2 + 4 * which)

    def gather_relay(v, which, far):
        for i in range(far):
            piece = at_block(v, xlo, (z + 8 - far_first(i)) % 8, core)
            arrived(piece, rgather.at[which, 4 + i])
            send(piece, piece, rgather.at[which, 3], beside, 2 + 4 * which)

    def gather_share(v, which, far):
        arrived(v.at[pl.ds(0, 4 * (7 - far))], rgather.at[which, 2])
        arrived(v.at[pl.ds(0, 28)], rgather.at[which, 3])
        half = v.at[pl.ds(core * 64, 64)]
        send(half, half, rgather.at[which, 1], sibling, 2 + 4 * which)

    def gather_finish(v, which):
        arrived(v.at[pl.ds(0, 64)], rgather.at[which, 1])

    def put_blocks(v, value):
        base = core * 64 + (xlo * 8 + z) * 4
        for b in range(4):
            v[base + b] = value[:, b * BLK : (b + 1) * BLK].astype(BF)

    def joined(ref):
        return ref[...].reshape(F, ROWS * BLK)

    def block_of(r, k):
        p = cols[r, k]
        return jnp.where(k < count[r], p // 4 % 2 * 64 + p // 8 * 4 + p % 4, NBLK)

    def product(v, rows):
        def step(q, totals):
            totals = list(totals)
            for n, r in enumerate(rows):
                for s in range(0, MINE, 2):
                    b = q * 8 + r % 2 * MINE + s
                    k = q * MINE + s
                    left = jnp.concatenate([v[block_of(r, k)], v[block_of(r, k + 1)]], axis=1)
                    right = jnp.concatenate([vals[r // 2][b], vals[r // 2][b + 1]], axis=1)
                    totals[n] = totals[n] + nt(left, right)
            return tuple(totals)

        zero = jnp.zeros((WIDE, BLK), F32)
        unroll = 4 if len(rows) > 2 else 8
        return lax.fori_loop(0, 8, step, (zero,) * len(rows), unroll=unroll)

    def term(g, pair, half, xl, i):
        p = dom_at(xl, (z + far_first(i)) % 8, half) * 4
        held, r = vals[pair], 2 * pair
        sums = []
        for b in range(0, 4, 2):
            right = jnp.concatenate(
                [
                    jnp.concatenate(
                        [held[inv[r + e, p + b]], held[inv[r + e, p + b + 1]]], axis=1
                    )
                    for e in range(2)
                ],
                axis=0,
            )
            got = jnp.dot(
                g[:, r * BLK : (r + 2) * BLK], right, preferred_element_type=F32
            )
            sums += [got[:, :BLK], got[:, BLK:]]
        return jnp.stack(sums)

    def over(at, n, write):
        def one(i, unused):
            write(i)
            return unused

        lax.fori_loop(at, at + n, one, 0, unroll=4)

    to_core, from_core, to_beside, from_beside, to_z, from_z, kept, early = bufs

    def first_rows(g):
        for n in range(4):
            half = 1 - core if n < 2 else core
            xl = xlo if n % 2 else 1 - xlo

            def one(i):
                early[n * 8 + i] = term(g, 0, half, xl, i)

            over(0, 8, one)

    def transposed(g, meanwhile):
        meanwhile[0]()
        for group in range(4):
            xl = 1 - xlo if group < 2 else xlo

            def one(i):
                at = group // 2 * 8 + i
                to_core[at] = (early[at] + term(g, 1, 1 - core, xl, i)).astype(BF)

            over(group % 2 * 4, 4, one)
            span = pl.ds(group * 4, 4)
            send(to_core.at[span], from_core.at[span], rred.at[group], sibling, 7)
        for group in range(4):
            if group % 2 == 0:
                arrived(from_core.at[pl.ds(group * 2, 4)], rred.at[group // 2])

            def two(i):
                total = early[16 + i] + term(g, 1, core, 1 - xlo, i)
                to_beside[i] = (total + from_core[i].astype(F32)).astype(BF)

            over(group * 2, 2, two)
            span = pl.ds(group * 2, 2)
            send(to_beside.at[span], from_beside.at[span], rred.at[4 + group], beside, 8)
        for group in range(2):
            arrived(from_core.at[pl.ds(8 + group * 4, 4)], rred.at[2 + group])

            def three(i):
                total = early[24 + i] + term(g, 1, core, xlo, i)
                kept[i] = total + from_core[8 + i].astype(F32)

            over(group * 4, 4, three)
        for group in range(4):
            if group == MEANWHILE:
                meanwhile[1]()
            arrived(from_beside.at[pl.ds(group * 2, 2)], rred.at[4 + group])
            for i in range(group * 2, group * 2 + 2):
                total = kept[i] + from_beside[i].astype(F32)
                if i < 7:
                    to_z[i] = total.astype(BF)
                    send(to_z.at[i], from_z.at[i], rred.at[8], along(far_first(i)), 9)
        kept[7] = total
        if MEANWHILE > 3:
            meanwhile[1]()
        total = kept[7]
        arrived(from_z.at[pl.ds(0, 7)], rred.at[8])
        for i in range(7):
            total = total + from_z[i].astype(F32)
        return jnp.concatenate([total[b] for b in range(4)], axis=1).astype(BF)

    zero_block = jnp.zeros((1, BLK, BLK), BF)
    vals[0][pl.ds(64, 1)] = zero_block
    vals[1][pl.ds(64, 1)] = zero_block
    v1[pl.ds(NBLK, 1)] = zero_block[:, :WIDE]
    v2[pl.ds(NBLK, 1)] = zero_block[:, :WIDE]
    hear_far()
    for copy in loads:
        copy.wait()
    put_blocks(v1, feats[...])
    pl.semaphore_wait(news.at[1], 2)
    gather_start(v1, 0, 0)
    lane = lax.broadcasted_iota(jnp.int32, (1, NBLK), 1)
    for r in range(ROWS):

        def mark(k, found):
            place = k // MINE * 8 + r % 2 * MINE + k % MINE - 64
            return found + jnp.where((lane == cols[r, k]) & (k < count[r]), place, 0)

        empty = jnp.full((1, NBLK), 64, jnp.int32)
        inv_rows[r : r + 1] = lax.fori_loop(0, 32, mark, empty, unroll=8)
    to_scalars = local(inv_rows, inv, 0)
    forward(below, 0, up)
    forward(above, 2, down)
    gather_second(v1, 0, 0)
    both_ways(0)
    forward(below, 1, up)
    forward(above, 3, down)
    forward(opposite, 0, across)
    forward(opposite, 2, across)
    w1_t[...] = w1[...].T
    w2_t[...] = w2[...].T
    both_ways(1)
    forward(opposite, 1, across)
    forward(opposite, 3, across)
    both_ways(2)
    both_ways(3)
    take(below, 3)
    take(above, 1)
    take(above, 0)
    take(below, 2)
    gather_share(v1, 0, 0)
    gather_finish(v1, 0)
    to_scalars.wait()

    def far_row(r):
        take(far_opposite, r)
        for n, q in enumerate((far_below, far_above)):
            take(q, r)

    def aggregate(rows):
        for r, total in zip(rows, product(v1, rows)):
            agg[c, :, r * BLK : (r + 1) * BLK] = total.astype(BF)

    far_row(0)
    far_row(1)
    aggregate((0, 1))
    cotangent = cot[...]
    first_rows(cotangent)
    far_row(2)
    aggregate((2,))
    far_row(3)
    mine = pl.ds(c * WIDE, WIDE)

    def last_row():
        aggregate((3,))
        spread(agg.at[c], agg, 0)

    def after_agg():
        collect(agg, 0)
        value = jnp.dot(w1_t[mine, :], joined(agg), preferred_element_type=F32)
        first[...] = value
        hid[c] = (value * jax.nn.sigmoid(value)).astype(BF)
        spread(hid.at[c], hid, 1)

    back[c] = transposed(cotangent, (last_row, after_agg))
    spread(back.at[c], back, 2)

    collect(hid, 1)
    put_blocks(v2, jnp.dot(w2_t[mine, :], joined(hid), preferred_element_type=F32))
    gather_start(v2, 1, 3)

    me = xlo * 2 + core
    pair = [
        (beside, (1 - xlo) * 2 + core),
        (sibling, xlo * 2 + 1 - core),
        (corner, (1 - xlo) * 2 + 1 - core),
    ]

    terms, quarters, along_z, whole = gbufs

    def quarters_out(n, grad):
        for k in range(4):
            terms[n, k] = grad[k * 8 : k * 8 + 8]
        for i, (to, k) in enumerate(pair):
            send(terms.at[n, k], quarters.at[n, i], rgrad.at[n], to, 10 + n)

    def sums_out():
        sums = []
        for n in range(2):
            total = terms[n, me]
            arrived(quarters.at[n], rgrad.at[n])
            for i in range(3):
                total = total + quarters[n, i]
            sums.append(total)
        along_z[7] = jnp.concatenate(sums, axis=0).astype(BF)
        for i in range(7):
            send(along_z.at[7], along_z.at[i], rgrad.at[2], along(far_first(i)), 12)

    def totals_out():
        arrived(along_z.at[pl.ds(0, 7)], rgrad.at[2])
        total = along_z[7].astype(F32)
        for i in range(7):
            total = total + along_z[i].astype(F32)
        whole[me] = total
        for to, k in pair:
            send(whole.at[me], whole.at[me], rgrad.at[3], to, 13)

    def totals_in():
        arrived(whole.at[pl.ds(0, 3)], rgrad.at[3])
        for k in range(4):
            for n in range(2):
                grads_ref[n, k * 8 : k * 8 + 8] = whole[k, n * 8 : n * 8 + 8]

    quarters_out(0, nt(back[c], joined(hid)))
    gather_second(v2, 1, 3)

    collect(back, 2)
    hidden_grad = jnp.dot(w2[mine, :], joined(back), preferred_element_type=F32)
    value = first[...]
    sig = jax.nn.sigmoid(value)
    act_grad = (hidden_grad * (sig + value * sig * (1.0 - sig))).astype(BF)
    quarters_out(1, nt(act_grad, joined(agg)))
    gather_relay(v2, 1, 3)
    sums_out()

    gather_share(v2, 1, 3)
    totals_out()
    gather_finish(v2, 1)
    for r, total in enumerate(product(v2, range(ROWS))):
        out_ref[:, r * BLK : (r + 1) * BLK] = total
    totals_in()
    sent(vals[0].at[pl.ds(0, 48)], 0)
    sent(vals[0].at[pl.ds(0, 64)], 1)
    sent(v1.at[pl.ds(0, 124)], 2)
    for n, full in enumerate((agg, hid, back)):
        sent(full.at[pl.ds(0, 7)], 3 + n)
    sent(v2.at[pl.ds(0, 124)], 6)
    sent(to_core, 7)
    sent(to_beside, 8)
    sent(to_z.at[pl.ds(0, 7)], 9)
    for n in range(2):
        sent(terms.at[n, pl.ds(0, 3)], 10 + n)
    sent(along_z.at[pl.ds(0, 7)], 12)
    sent(whole.at[pl.ds(0, 3)], 13)


def body(feats, w_first, w_second, block_cols, block_count, block_vals, cotangent):
    def blocks(n, kind):
        return pltpu.VMEM((n, 4, WIDE, BLK), kind)

    reduce_bufs = [blocks(n, BF) for n in (16, 16, 8, 8, 8, 8)]
    grad_bufs = [
        pltpu.VMEM((2, 4, 8, F), F32),
        pltpu.VMEM((2, 3, 8, F), F32),
        pltpu.VMEM((8, 16, F), BF),
        pltpu.VMEM((4, 16, F), F32),
    ]
    vmem = pl.BlockSpec(memory_space=pltpu.VMEM)
    anywhere = pl.BlockSpec(memory_space=pl.ANY)
    wide = pltpu.VMEM((8, WIDE, ROWS * BLK), BF)
    square = pltpu.VMEM((F, F), BF)
    dma = pltpu.SemaphoreType.DMA
    out, grads = pl.pallas_call(
        kernel,
        out_shape=(
            jax.ShapeDtypeStruct((WIDE, ROWS * BLK), F32),
            jax.ShapeDtypeStruct((2, WIDE, F), F32),
        ),
        in_specs=[anywhere] * 7,
        out_specs=(vmem, vmem),
        scratch_shapes=[
            [pltpu.VMEM((NBLK // 2 + 1, BLK, BLK), BF)] * 2,
            pltpu.VMEM((WIDE, ROWS * BLK), BF),
            wide,
            wide,
            wide,
            pltpu.VMEM((WIDE, ROWS * BLK), F32),
            pltpu.VMEM((NBLK + 1, WIDE, BLK), BF),
            pltpu.VMEM((NBLK + 1, WIDE, BLK), BF),
            square,
            square,
            square,
            square,
            pltpu.VMEM((WIDE, ROWS * BLK), BF),
            pltpu.VMEM((ROWS, NBLK), jnp.int32),
            pltpu.SMEM((ROWS, 32), jnp.int32),
            pltpu.SMEM((ROWS,), jnp.int32),
            pltpu.SMEM((ROWS, NBLK), jnp.int32),
            reduce_bufs + [blocks(8, F32), blocks(32, F32)],
            grad_bufs,
            dma((14,)),
            dma((8, 4)),
            dma((3,)),
            dma((2, 7)),
            dma((9,)),
            dma((4,)),
            dma((8,)),
            dma((2,)),
            pltpu.SemaphoreType.REGULAR((2,)),
        ],
        compiler_params=pltpu.CompilerParams(
            collective_id=0, has_side_effects=True, vmem_limit_bytes=56 << 20
        ),
        name="graph_layers",
    )(
        feats.T,
        cotangent.T,
        w_first,
        w_second,
        block_vals.reshape(ROWS * MINE, BLK, BLK),
        block_cols,
        block_count,
    )
    return (out.T, grads[1].T, grads[0].T)


def solution(mesh):
    return jax.shard_map(
        body,
        mesh=mesh,
        in_specs=(
            P("dom", "col"),
            P(),
            P(),
            P("dom", None),
            P("dom"),
            P("dom", "col", None, None),
            P("dom", "col"),
        ),
        out_specs=(P("dom", "col"), P(None, "col"), P(None, "col")),
        check_vma=False,
    )
```

time: 80.6 us -> 77.1 us (0.957)
  Pallas kernels: 77.7 us -> 74.3 us
    pallas_call x1, Pallas kernels: 77.7 us -> 74.3 us  [body(): pl.pallas_call(kernel, out_shape=(jax.ShapeDtypeStruct((WIDE, ROWS * BLK)...]
where the time goes in v4:
time: 77.1 us; the launch traced here: 77 us
  Pallas kernels  74.3 us (96%)
  local copies, waits for them, and re-layouts  2.07 us (3%)
    pallas_call x1, Pallas kernels, body(): pl.pallas_call(kernel, out_shape=(jax.ShapeDtypeStruct((WIDE, ROWS * BLK)...  74.3 us

profile of v4, /device:TPU:1, one launch (start us, length us, event | category | flops | bytes accessed | tf_op | source)
XLA Modules:
  0.0 77.0 jit_solution(14823330686851174170)
XLA Ops:
  0.6 74.3 %graph_layers.1 = (f32[32,512]{1,0:T(8,128)}, f32[2,32,256]{2,1,0:T(8,128)}) custom-call(bf16[32,512]{1,0:T(8,128)(2,1)} %bitcast.14, bf16[32,512]{1,0:T(8,128)(2,1)} %bitcast.15, bf16[256,256]{1,0:T(8,128)(2,1)} %w1_in.1, bf16[256,256]{1,0:T(8,128)(2,1)} %w2_in.1, bf16[16,128,128]{2,1,0:T(8,128)(2,1)} %bitcast.12, s32[4,32]{1,0:T(4,128)} %cols_in.1, s32[4]{0:T(128)} %count_in.1), custom_call_target="tpu_custom_call" | custom-call | tf_op jit(solution)/shard_map/graph_layers/pallas_call | solution.py:513
  74.9 0.0 copy-start
  74.9 1.4 %slice_bitcast_fusion = (f32[256,32]{0,1:T(8,128)}, f32[256,32]{0,1:T(8,128)}) fusion(f32[2,32,256]{2,1,0:T(8,128)} %get-tuple-element.6), kind=kLoop, calls=%fused_computation | loop fusion | bytes 131072 | tf_op jit(solution)/shard_map/transpose | solution.py:564
  76.3 0.0 copy-done
  76.3 0.6 copy.11
Async XLA Ops:
  74.9 1.4 %copy-start = (f32[32,512]{1,0:T(8,128)S(1)}, f32[32,512]{1,0:T(8,128)}, u32[]{:S(2)}) copy-start(f32[32,512]{1,0:T(8,128)} %get-tuple-element.5) | copy-start | bytes 196612

commit v5 on v4

--- a/solution.py
+++ b/solution.py
@@ -164,9 +164,11 @@
     def send_own(r, to):
         send(vals_in.at[pl.ds(r * MINE, MINE)], part(c, r), rvals.at[c, r], to, 0)
 
-    for r in range(ROWS):
+    for r in range(2):
         send_own(r, up)
-        send_own((2, 3, 0, 1)[r], down)
+        send_own(2 + r, down)
+        send_own(r, across)
+    for r in range(2, 4):
         send_own(r, across)
 
     below, above = col_at(xhi, y + 3), col_at(xhi, y + 1)
@@ -188,6 +190,8 @@
     def both_ways(r):
         take(partner, r)
         piece = part(partner, r)
+        if r == 3:
+            piece = piece.at[pl.ds(0, 2)]
         send(piece, piece, rvals.at[partner, r], up, 1)
         send(piece, piece, rvals.at[partner, r], down, 1)
 
@@ -361,20 +365,25 @@
     to_scalars = local(inv_rows, inv, 0)
     forward(below, 0, up)
     forward(above, 2, down)
+    forward(below, 1, up)
+    forward(above, 3, down)
+    for r in range(2):
+        send_own(2 + r, up)
+        send_own(r, down)
     gather_second(v1, 0, 0)
     both_ways(0)
-    forward(below, 1, up)
-    forward(above, 3, down)
     forward(opposite, 0, across)
     forward(opposite, 2, across)
+    both_ways(1)
     w1_t[...] = w1[...].T
     w2_t[...] = w2[...].T
-    both_ways(1)
     forward(opposite, 1, across)
     forward(opposite, 3, across)
     both_ways(2)
     both_ways(3)
     take(below, 3)
+    send(second_half(below), second_half(below), rhalf.at[0], across, 14)
+    send(second_half(above), second_half(above), rhalf.at[1], across, 14)
     take(above, 1)
     take(above, 0)
     take(below, 2)
@@ -385,7 +394,11 @@
     def far_row(r):
         take(far_opposite, r)
         for n, q in enumerate((far_below, far_above)):
-            take(q, r)
+            if r == 3:
+                arrived(vals[1].at[pl.ds(q * 8 + MINE, 2)], rvals.at[q, r])
+                arrived(second_half(q), rhalf.at[n])
+            else:
+                take(q, r)
 
     def aggregate(rows):
         for r, total in zip(rows, product(v1, rows)):
@@ -480,7 +493,8 @@
         out_ref[:, r * BLK : (r + 1) * BLK] = total
     totals_in()
     sent(vals[0].at[pl.ds(0, 48)], 0)
-    sent(vals[0].at[pl.ds(0, 64)], 1)
+    sent(vals[0].at[pl.ds(0, 60)], 1)
+    sent(vals[0].at[pl.ds(0, 4)], 14)
     sent(v1.at[pl.ds(0, 124)], 2)
     for n, full in enumerate((agg, hid, back)):
         sent(full.at[pl.ds(0, 7)], 3 + n)
@@ -538,7 +552,7 @@
             pltpu.SMEM((ROWS, NBLK), jnp.int32),
             reduce_bufs + [blocks(8, F32), blocks(32, F32)],
             grad_bufs,
-            dma((14,)),
+            dma((15,)),
             dma((8, 4)),
             dma((3,)),
             dma((2, 7)),

time: 77.1 us -> 75.4 us (0.978)
  Pallas kernels: 74.3 us -> 72.6 us
    pallas_call x1, Pallas kernels: 74.3 us -> 72.6 us  [body(): pl.pallas_call(kernel, out_shape=(jax.ShapeDtypeStruct((WIDE, ROWS * BLK)...]
where the time goes in v5:
time: 75.4 us; the launch traced here: 75.3 us
  Pallas kernels  72.6 us (96%)
  local copies, waits for them, and re-layouts  2.07 us (3%)
    pallas_call x1, Pallas kernels, body(): pl.pallas_call(kernel, out_shape=(jax.ShapeDtypeStruct((WIDE, ROWS * BLK)...  72.6 us

profile of v5, /device:TPU:1, one launch (start us, length us, event | category | flops | bytes accessed | tf_op | source)
XLA Modules:
  0.0 75.3 jit_solution(3893714565492076332)
XLA Ops:
  0.6 72.6 %graph_layers.1 = (f32[32,512]{1,0:T(8,128)}, f32[2,32,256]{2,1,0:T(8,128)}) custom-call(bf16[32,512]{1,0:T(8,128)(2,1)} %bitcast.14, bf16[32,512]{1,0:T(8,128)(2,1)} %bitcast.15, bf16[256,256]{1,0:T(8,128)(2,1)} %w1_in.1, bf16[256,256]{1,0:T(8,128)(2,1)} %w2_in.1, bf16[16,128,128]{2,1,0:T(8,128)(2,1)} %bitcast.12, s32[4,32]{1,0:T(4,128)} %cols_in.1, s32[4]{0:T(128)} %count_in.1), custom_call_target="tpu_custom_call" | custom-call | tf_op jit(solution)/shard_map/graph_layers/pallas_call | solution.py:527
  73.2 0.0 copy-start
  73.2 1.4 %slice_bitcast_fusion = (f32[256,32]{0,1:T(8,128)}, f32[256,32]{0,1:T(8,128)}) fusion(f32[2,32,256]{2,1,0:T(8,128)} %get-tuple-element.6), kind=kLoop, calls=%fused_computation | loop fusion | bytes 131072 | tf_op jit(solution)/shard_map/transpose | solution.py:578
  74.7 0.0 copy-done
  74.7 0.6 copy.11
Async XLA Ops:
  73.2 1.4 %copy-start = (f32[32,512]{1,0:T(8,128)S(1)}, f32[32,512]{1,0:T(8,128)}, u32[]{:S(2)}) copy-start(f32[32,512]{1,0:T(8,128)} %get-tuple-element.5) | copy-start | bytes 196612

commit v6 on v5

--- a/solution.py
+++ b/solution.py
@@ -11,7 +11,7 @@
 ROWS = 4
 MINE = 4
 NBLK = 128
-MEANWHILE = 4
+MEANWHILE = 3
 WIDE = 32
 F = 256
 MESH = pl.DeviceIdType.MESH
@@ -36,7 +36,6 @@
     cols_in,
     count_in,
     out_ref,
-    grads_ref,
     vals,
     feats,
     agg,
@@ -472,7 +471,7 @@
         arrived(whole.at[pl.ds(0, 3)], rgrad.at[3])
         for k in range(4):
             for n in range(2):
-                grads_ref[n, k * 8 : k * 8 + 8] = whole[k, n * 8 : n * 8 + 8]
+                out_ref[k * 8 : k * 8 + 8, ROWS * BLK + n * F : ROWS * BLK + n * F + F] = whole[k, n * 8 : n * 8 + 8]
 
     quarters_out(0, nt(back[c], joined(hid)))
     gather_second(v2, 1, 3)
@@ -524,14 +523,13 @@
     wide = pltpu.VMEM((8, WIDE, ROWS * BLK), BF)
     square = pltpu.VMEM((F, F), BF)
     dma = pltpu.SemaphoreType.DMA
-    out, grads = pl.pallas_call(
+    (out,) = pl.pallas_call(
         kernel,
         out_shape=(
-            jax.ShapeDtypeStruct((WIDE, ROWS * BLK), F32),
-            jax.ShapeDtypeStruct((2, WIDE, F), F32),
+            jax.ShapeDtypeStruct((WIDE, ROWS * BLK + 2 * F), F32),
         ),
         in_specs=[anywhere] * 7,
-        out_specs=(vmem, vmem),
+        out_specs=(vmem,),
         scratch_shapes=[
             [pltpu.VMEM((NBLK // 2 + 1, BLK, BLK), BF)] * 2,
             pltpu.VMEM((WIDE, ROWS * BLK), BF),
@@ -575,7 +573,8 @@
         block_cols,
         block_count,
     )
-    return (out.T, grads[1].T, grads[0].T)
+    at = ROWS * BLK
+    return (out[:, :at].T, out[:, at + F :].T, out[:, at : at + F].T)
 
 
 def solution(mesh):

time: 75.4 us -> 75.5 us (level)
    transpose x1 -> x2, local copies, waits for them, and re-layouts: 1.44 us -> 2.09 us  [body(): return (out[:, :at].T, out[:, at + F:].T, out[:, at:at + F].T)]
where the time goes in v6:
time: 75.5 us; the launch traced here: 75.4 us
  Pallas kernels  72.6 us (96%)
  local copies, waits for them, and re-layouts  2.09 us (3%)
    pallas_call x1, Pallas kernels, body(): pl.pallas_call(kernel, out_shape=(jax.ShapeDtypeStruct((WIDE, ROWS * BLK...  72.6 us
    transpose x2, local copies, waits for them, and re-layouts, body(): return (out[:, :at].T, out[:, at + F:].T, out[:, at:at + F].T)  2.09 us

profile of v6, /device:TPU:1, one launch (start us, length us, event | category | flops | bytes accessed | tf_op | source)
XLA Modules:
  0.0 75.4 jit_solution(4488246997512412125)
XLA Ops:
  0.6 72.6 %graph_layers.1 = f32[32,1024]{1,0:T(8,128)} custom-call(bf16[32,512]{1,0:T(8,128)(2,1)} %bitcast.10, bf16[32,512]{1,0:T(8,128)(2,1)} %bitcast.11, bf16[256,256]{1,0:T(8,128)(2,1)} %w1_in.1, bf16[256,256]{1,0:T(8,128)(2,1)} %w2_in.1, bf16[16,128,128]{2,1,0:T(8,128)(2,1)} %bitcast.9, s32[4,32]{1,0:T(4,128)} %cols_in.1, s32[4]{0:T(128)} %count_in.1), custom_call_target="tpu_custom_call" | custom-call | tf_op jit(solution)/shard_map/graph_layers/pallas_call | solution.py:526
  73.3 0.0 copy-start
  73.3 1.5 %slice_bitcast_fusion.1 = (f32[256,32]{0,1:T(8,128)}, f32[256,32]{0,1:T(8,128)}) fusion(f32[32,1024]{1,0:T(8,128)} %graph_layers.1), kind=kLoop, calls=%fused_computation.1 | loop fusion | bytes 131072 | tf_op jit(solution)/shard_map/transpose | solution.py:577
  74.7 0.0 copy-done
  74.7 0.6 slice_bitcast_fusion
Async XLA Ops:
  73.3 1.5 %copy-start = (f32[32,1024]{1,0:T(8,128)S(1)}, f32[32,1024]{1,0:T(8,128)}, u32[]{:S(2)}) copy-start(f32[32,1024]{1,0:T(8,128)} %graph_layers.1) | copy-start | bytes 393220
